TPU v7x, 256 devices: a whole 4x4x8 slice. The times are simulated.
256 devices in a mesh: ham: 32 (over z, y_hi, core), walk: 8 (over x, y_lo).
Axes of the slice: x: 4, y: 4 (y_hi: 2, y_lo: 2; y = y_hi * 2 + y_lo), z: 8, core: 2. Of those that a mesh axis runs over, the one named last changes fastest.
Arguments:
- chol: bfloat16 [128, 256, 1024], P('ham'), may hold values from -0.1875 to 0.1875
- green: bfloat16 [1024, 1024, 256], P(('walk', 'ham')), may hold values from -6 to 6
- fields: float32 [1024, 16], P(('walk', 'ham')), may hold values from -5 to 5
- weights_in: float32 [1024], P(('walk', 'ham')), may hold values from 0.5 to 2
- partner: int32 [1024], P(('walk', 'ham')), may hold values from 0 to 1023, as said below
- counts: int32 [8, 32], P('walk', 'ham'), may hold values from 1 to 4, as said below
Outputs:
- paired_weights: float32 [1024], P(('walk', 'ham'))
- local_energy: float32 [1024], P(('walk', 'ham'))
- force_bias: float32 [1024, 16], P(('walk', 'ham'))
- energy_mean: float32 [], replicated
Inputs may be any that keep to these rules, and one draw needn't show every extreme that they name: partner[partner[w]] = w; partner[w] lies in another group than w, at the same slab position (w // 4) % 32; all walkers of one group are matched into one group. `counts`: some entry equals 4.
All inputs are finite; a program needn't handle non-finite values.
Results may differ from a plain program's by a relative error of at most 0.0003.
Values may be sent and summed in bfloat16 or wider, within the bound.
A program may use at most 128 MiB of HBM per device.

v0:
```python
import jax
import jax.numpy as jnp
from jax import lax
from jax.sharding import PartitionSpec as P

NOCC = 256
CHOL_DEV = 4
STOPS = 4


FIELD_COUPLING = 0.02
DRIFT_COST = 0.0002
ONE_BODY = 1.0


def from_behind(block, axis, distance):
    devices = range(lax.axis_size(axis))
    route = [((i - distance) % len(devices), i) for i in devices]
    return lax.ppermute(block, axis, route)


def stop_terms(slab, theta):
    prod = jnp.einsum("vik,bkj->bvij", slab, theta, preferred_element_type=jnp.float32)
    bias_part = jnp.trace(prod, axis1=2, axis2=3)
    exchange_part = jnp.sum(prod * jnp.swapaxes(prod, 2, 3), axis=(1, 2, 3))
    return (bias_part, exchange_part)


def body(chol, green, fields, weights_in, partner, counts):
    walkers_here = green.shape[0]
    bias_list = []
    exchange_total = jnp.zeros((walkers_here,), jnp.float32)
    for offset in range(-1, STOPS - 1):
        if offset == 0:
            bias_part, exchange_part = stop_terms(chol, green)
        else:
            visitor = from_behind(green, "ham", offset)
            bias_far, exchange_far = stop_terms(chol, visitor)
            bias_part, exchange_part = from_behind((bias_far, exchange_far), "ham", -offset)
        bias_list.append(bias_part)
        exchange_total = exchange_total + exchange_part
    force_bias = jnp.concatenate(bias_list, axis=1)
    squares = jnp.sum(force_bias * force_bias, axis=1)
    local_energy = ONE_BODY + (0.5 * squares - 0.5 * exchange_total) / (NOCC * STOPS * CHOL_DEV)
    size_walk = lax.axis_size("walk")
    group_slots = lax.axis_size("ham") * walkers_here
    live = (jnp.arange(walkers_here) < counts[0, 0]).astype(jnp.float32)
    log_ratio = FIELD_COUPLING * jnp.sum(fields * force_bias, axis=1) - DRIFT_COST * squares
    new_weight = weights_in * jnp.exp(log_ratio) * live
    everyone = lax.all_gather(new_weight, "walk", axis=0, tiled=True)
    flat_index = partner // group_slots * walkers_here + partner % walkers_here
    picker = flat_index[:, None] == jnp.arange(size_walk * walkers_here)[None, :]
    mate_weight = jnp.sum(jnp.where(picker, everyone[None, :], 0.0), axis=1)
    paired_weights = 0.5 * (new_weight + mate_weight)
    numer, denom = lax.psum(
        (jnp.sum(new_weight * local_energy), jnp.sum(new_weight)), ("ham", "walk")
    )
    return (paired_weights, local_energy, force_bias, numer / denom)


def solution(mesh):
    placed = (
        P("ham", None, None),
        P(("walk", "ham"), None, None),
        P(("walk", "ham"), None),
        P(("walk", "ham")),
        P(("walk", "ham")),
        P("walk", "ham"),
    )
    return jax.shard_map(
        body,
        mesh=mesh,
        in_specs=placed,
        out_specs=(P(("walk", "ham")), P(("walk", "ham")), P(("walk", "ham"), None), P()),
        check_vma=False,
    )
```

profile of v0, /device:TPU:1, one launch (start us, length us, event | category | flops | bytes accessed | tf_op | source)
XLA Modules:
  0.0 260.6 jit_solution(7209522400453342584)
XLA Ops:
  0.6 0.0 copy-start
  0.6 4.2 %copy.18 = bf16[4,1024,256]{1,2,0:T(8,128)(2,1)} copy(bf16[4,1024,256]{2,1,0:T(8,128)(2,1)} %param.7) | data formatting | bytes 4194304 | tf_op args[1]
  4.8 3.2 %collective-permute-start = (bf16[4,1024,256]{1,2,0:T(8,128)(2,1)}, bf16[4,1024,256]{1,2,0:T(8,128)(2,1)}, u32[]{:S(2)}, u32[]{:S(2)}) collective-permute-start(bf16[4,1024,256]{1,2,0:T(8,128)(2,1)} %copy.18), channel_id=1, source_target_pairs={{8,0},{16,8},{24,16},{32,24},{40,32},{48,40},{56,48},{64,56},{72,6... | collective-permute-start | bytes 6291464 | tf_op jit(solution)/shard_map/ppermute | solution.py:19
  8.1 1.1 collective-permute-start.2
  9.1 3.6 %collective-permute-start.4 = (bf16[4,1024,256]{1,2,0:T(8,128)(2,1)}, bf16[4,1024,256]{1,2,0:T(8,128)(2,1)}, u32[]{:S(2)}, u32[]{:S(2)}) collective-permute-start(bf16[4,1024,256]{1,2,0:T(8,128)(2,1)} %copy.18), channel_id=1, source_target_pairs={{240,0},{248,8},{0,16},{8,24},{16,32},{24,40},{32,48},{40,56},{48,... | collective-permute-start | bytes 6291464 | tf_op jit(solution)/shard_map/ppermute | solution.py:19
  12.7 0.0 copy-done
  12.7 5.9 %fusion.8 = f32[4,256,4,256]{3,1,2,0:T(8,128)} fusion(bf16[4,1024,256]{2,1,0:T(8,128)(2,1)} %param.7, bf16[4,256,1024]{2,1,0:T(8,128)(2,1)S(1)} %copy-done), kind=kOutput, calls=%fused_computation.16 | convolution fusion | flops 2147483648 | bytes 8388608 | tf_op jit(solution)/shard_map/vik,bkj->bvij/dot_general | solution.py:23
  18.6 0.0 copy-start.4
  18.6 0.0 copy-start.3
  18.6 5.3 %copy.21 = f32[4,256,4,256]{1,3,2,0:T(8,128)} copy(f32[4,256,4,256]{3,1,2,0:T(8,128)} %fusion.8) | data formatting | bytes 8388608 | tf_op jit(solution)/shard_map/vik,bkj->bvij/dot_general | solution.py:23
  24.5 0.0 copy-done.4
  24.5 0.6 dynamic-slice
  25.8 0.0 copy-done.3
  25.8 74.7 %collective-permute-done = bf16[4,1024,256]{1,2,0:T(8,128)(2,1)} collective-permute-done((bf16[4,1024,256]{1,2,0:T(8,128)(2,1)}, bf16[4,1024,256]{1,2,0:T(8,128)(2,1)}, u32[]{:S(2)}, u32[]{:S(2)}) %collective-permute-start) | collective-permute-done | bytes 2097184 | tf_op jit(solution)/shard_map/ppermute | solution.py:19
  100.6 5.9 %fusion.14 = f32[4,256,4,256]{3,1,2,0:T(8,128)} fusion(bf16[4,1024,256]{1,2,0:T(8,128)(2,1)} %collective-permute-done, bf16[4,256,1024]{2,1,0:T(8,128)(2,1)S(1)} %copy-done), kind=kOutput, calls=%fused_computation.22 | convolution fusion | flops 2147483648 | bytes 8388608 | tf_op jit(solution)/shard_map/vik,bkj->bvij/dot_general | solution.py:23
  106.5 5.2 %copy.19 = f32[4,256,4,256]{1,3,2,0:T(8,128)} copy(f32[4,256,4,256]{3,1,2,0:T(8,128)} %fusion.14) | data formatting | bytes 8388608 | tf_op jit(solution)/shard_map/vik,bkj->bvij/dot_general | solution.py:23
  111.7 0.0 collective-permute-done.2
  111.7 5.9 %fusion.12 = f32[4,256,4,256]{3,1,2,0:T(8,128)} fusion(bf16[4,1024,256]{1,2,0:T(8,128)(2,1)} %collective-permute-done.2, bf16[4,256,1024]{2,1,0:T(8,128)(2,1)S(1)} %copy-done), kind=kOutput, calls=%fused_computation.20 | convolution fusion | flops 2147483648 | bytes 8388608 | tf_op jit(solution)/shard_map/vik,bkj->bvij/dot_general | solution.py:23
  117.7 5.2 %copy.23 = f32[4,256,4,256]{1,3,2,0:T(8,128)} copy(f32[4,256,4,256]{3,1,2,0:T(8,128)} %fusion.12) | data formatting | bytes 8388608 | tf_op jit(solution)/shard_map/vik,bkj->bvij/dot_general | solution.py:23
  122.9 0.0 collective-permute-done.4
  122.9 5.9 %fusion.10 = f32[4,256,4,256]{3,1,2,0:T(8,128)} fusion(bf16[4,1024,256]{1,2,0:T(8,128)(2,1)} %collective-permute-done.4, bf16[4,256,1024]{2,1,0:T(8,128)(2,1)S(1)} %copy-done), kind=kOutput, calls=%fused_computation.18 | convolution fusion | flops 2147483648 | bytes 8388608 | tf_op jit(solution)/shard_map/vik,bkj->bvij/dot_general | solution.py:23
  128.8 5.3 %copy.25 = f32[4,256,4,256]{1,3,2,0:T(8,128)} copy(f32[4,256,4,256]{3,1,2,0:T(8,128)} %fusion.10) | data formatting | bytes 8388608 | tf_op jit(solution)/shard_map/vik,bkj->bvij/dot_general | solution.py:23
  134.1 0.0 copy-start.1
  134.1 0.0 copy-start.2
  134.1 12.3 %fusion.2 = (f32[4]{0:T(128)S(1)}, f32[4,4]{1,0:T(4,128)S(1)}, f32[4,4]{1,0:T(4,128)S(1)}, f32[4]{0:T(128)S(1)}, f32[4,4]{1,0:T(4,128)S(1)}, /*index=5*/f32[4]{0:T(128)S(1)}, f32[4,4]{1,0:T(4,128)S(1)}, f32[4]{0:T(128)S(1)}) fusion(f32[4,256,4,256]{3,1,2,0:T(8,128)} %fusion.8, f32[4,256,4,256]{1,3,2,0:T(8,128)} %copy.21, ...), kind=kLoop, calls=%fused_computation.5 | loop fusion | flops 16777136 | bytes 33620288 | tf_op jit(solution)/shard_map/reduce_sum | solution.py:25
  146.4 0.1 collective-permute-start.1
  146.5 0.5 collective-permute-start.3
  147.0 5.0 %collective-permute-start.5 = (f32[4,4]{1,0:T(4,128)S(1)}, f32[4,4]{1,0:T(4,128)S(1)}, u32[]{:S(2)}, u32[]{:S(2)}) collective-permute-start(f32[4,4]{1,0:T(4,128)S(1)} %get-tuple-element.23), channel_id=1, source_target_pairs={{16,0},{24,8},{32,16},{40,24},{48,32},{56,40},{64,48},{72,56},{80,... | collective-permute-start | bytes 200 | tf_op jit(solution)/shard_map/ppermute | solution.py:19
  152.0 0.0 collective-permute-start.6
  152.0 3.7 %collective-permute-start.7 = (f32[4]{0:T(128)S(1)}, f32[4]{0:T(128)S(1)}, u32[]{:S(2)}, u32[]{:S(2)}) collective-permute-start(f32[4]{0:T(128)S(1)} %get-tuple-element.22), channel_id=1, source_target_pairs={{8,0},{16,8},{24,16},{32,24},{40,32},{48,40},{56,48},{64,56},{72,6... | collective-permute-start | bytes 56 | tf_op jit(solution)/shard_map/ppermute | solution.py:19
  155.7 0.0 collective-permute-done.1
  155.7 5.0 %collective-permute-start.8 = (f32[4]{0:T(128)S(1)}, f32[4]{0:T(128)S(1)}, u32[]{:S(2)}, u32[]{:S(2)}) collective-permute-start(f32[4]{0:T(128)S(1)} %get-tuple-element.24), channel_id=1, source_target_pairs={{16,0},{24,8},{32,16},{40,24},{48,32},{56,40},{64,48},{72,56},{80,... | collective-permute-start | bytes 56 | tf_op jit(solution)/shard_map/ppermute | solution.py:19
  160.7 0.0 collective-permute-done.3
  160.7 0.0 collective-permute-done.5
  160.7 0.0 copy-done.1
  160.7 0.8 multiply_reduce_fusion.1
  161.5 0.0 collective-permute-done.6
  161.5 0.0 collective-permute-done.7
  161.6 0.0 collective-permute-done.8
  161.6 0.0 copy-done.2
  161.6 1.2 fusion.21
  162.8 0.2 dynamic-update-slice
  163.0 15.7 %all-reduce = f32[32]{0:T(128)S(1)} all-reduce(f32[32]{0:T(128)S(1)} %dynamic-update-slice), channel_id=1, replica_groups=mesh['ham'=32,'walk'=8] {'walk'}, use_global_device_ids=true, to_apply=%add | all-reduce | flops 32 | bytes 256
  178.7 0.2 select_reduce_fusion
  178.9 0.5 add_multiply_fusion
  179.4 78.8 %all-reduce.1 = (f32[]{:T(128)}, f32[]{:T(128)}) all-reduce(f32[]{:T(128)} %get-tuple-element.15, f32[]{:T(128)} %get-tuple-element.14), channel_id=1, replica_groups=mesh['ham'=32,'walk'=8] {'ham','walk'}, use_global_device_ids=true, to_apply=%region_12.13 | all-reduce | flops 2 | bytes 16 | tf_op jit(solution)/shard_map/psum | solution.py:55
  (3 shorter events, 0.0 us)
Async XLA Ops:
  0.6 12.1 %copy-start = (bf16[4,256,1024]{2,1,0:T(8,128)(2,1)S(1)}, bf16[4,256,1024]{2,1,0:T(8,128)(2,1)}, u32[]{:S(2)}) copy-start(bf16[4,256,1024]{2,1,0:T(8,128)(2,1)} %param.6) | copy-start | bytes 6291460
  4.8 95.7 %collective-permute-start = (bf16[4,1024,256]{1,2,0:T(8,128)(2,1)}, bf16[4,1024,256]{1,2,0:T(8,128)(2,1)}, u32[]{:S(2)}, u32[]{:S(2)}) collective-permute-start(bf16[4,1024,256]{1,2,0:T(8,128)(2,1)} %copy.18), channel_id=1, source_target_pairs={{8,0},{16,8},{24,16},{32,24},{40,32},{48,40},{56,48},{64,56},{72,6... | collective-permute-start | bytes 6291464 | tf_op jit(solution)/shard_map/ppermute | solution.py:19
  8.1 103.7 %collective-permute-start.2 = (bf16[4,1024,256]{1,2,0:T(8,128)(2,1)}, bf16[4,1024,256]{1,2,0:T(8,128)(2,1)}, u32[]{:S(2)}, u32[]{:S(2)}) collective-permute-start(bf16[4,1024,256]{1,2,0:T(8,128)(2,1)} %copy.18), channel_id=1, source_target_pairs={{248,0},{0,8},{8,16},{16,24},{24,32},{32,40},{40,48},{48,56},{56,6... | collective-permute-start | bytes 6291464 | tf_op jit(solution)/shard_map/ppermute | solution.py:19
  9.1 113.8 %collective-permute-start.4 = (bf16[4,1024,256]{1,2,0:T(8,128)(2,1)}, bf16[4,1024,256]{1,2,0:T(8,128)(2,1)}, u32[]{:S(2)}, u32[]{:S(2)}) collective-permute-start(bf16[4,1024,256]{1,2,0:T(8,128)(2,1)} %copy.18), channel_id=1, source_target_pairs={{240,0},{248,8},{0,16},{8,24},{16,32},{24,40},{32,48},{40,56},{48,... | collective-permute-start | bytes 6291464 | tf_op jit(solution)/shard_map/ppermute | solution.py:19
  18.6 5.9 %copy-start.4 = (u32[256]{0:T(256)S(1)}, u32[256]{0:T(256)}, u32[]{:S(2)}) copy-start(u32[256]{0:T(256)} %constant.63) | copy-start | bytes 3076
  18.6 7.2 %copy-start.3 = (s32[4]{0:T(128)S(1)}, s32[4]{0:T(128)}, u32[]{:S(2)}) copy-start(s32[4]{0:T(128)} %param.10) | copy-start | bytes 52
  134.1 26.6 %copy-start.1 = (f32[4,16]{1,0:T(4,128)S(1)}, f32[4,16]{1,0:T(4,128)}, u32[]{:S(2)}) copy-start(f32[4,16]{1,0:T(4,128)} %param.8) | copy-start | bytes 772
  134.1 27.5 %copy-start.2 = (f32[4]{0:T(128)S(1)}, f32[4]{0:T(128)}, u32[]{:S(2)}) copy-start(f32[4]{0:T(128)} %param.9) | copy-start | bytes 52
  146.4 9.3 %collective-permute-start.1 = (f32[4,4]{1,0:T(4,128)S(1)}, f32[4,4]{1,0:T(4,128)S(1)}, u32[]{:S(2)}, u32[]{:S(2)}) collective-permute-start(f32[4,4]{1,0:T(4,128)S(1)} %get-tuple-element.25), channel_id=1, source_target_pairs={{248,0},{0,8},{8,16},{16,24},{24,32},{32,40},{40,48},{48,56},{56,6... | collective-permute-start | bytes 200 | tf_op jit(solution)/shard_map/ppermute | solution.py:19
  146.5 14.2 %collective-permute-start.3 = (f32[4,4]{1,0:T(4,128)S(1)}, f32[4,4]{1,0:T(4,128)S(1)}, u32[]{:S(2)}, u32[]{:S(2)}) collective-permute-start(f32[4,4]{1,0:T(4,128)S(1)} %get-tuple-element.21), channel_id=1, source_target_pairs={{8,0},{16,8},{24,16},{32,24},{40,32},{48,40},{56,48},{64,56},{72,6... | collective-permute-start | bytes 200 | tf_op jit(solution)/shard_map/ppermute | solution.py:19
  147.0 13.7 %collective-permute-start.5 = (f32[4,4]{1,0:T(4,128)S(1)}, f32[4,4]{1,0:T(4,128)S(1)}, u32[]{:S(2)}, u32[]{:S(2)}) collective-permute-start(f32[4,4]{1,0:T(4,128)S(1)} %get-tuple-element.23), channel_id=1, source_target_pairs={{16,0},{24,8},{32,16},{40,24},{48,32},{56,40},{64,48},{72,56},{80,... | collective-permute-start | bytes 200 | tf_op jit(solution)/shard_map/ppermute | solution.py:19
  152.0 9.5 %collective-permute-start.6 = (f32[4]{0:T(128)S(1)}, f32[4]{0:T(128)S(1)}, u32[]{:S(2)}, u32[]{:S(2)}) collective-permute-start(f32[4]{0:T(128)S(1)} %get-tuple-element.26), channel_id=1, source_target_pairs={{248,0},{0,8},{8,16},{16,24},{24,32},{32,40},{40,48},{48,56},{56,6... | collective-permute-start | bytes 56 | tf_op jit(solution)/shard_map/ppermute | solution.py:19
  152.0 9.5 %collective-permute-start.7 = (f32[4]{0:T(128)S(1)}, f32[4]{0:T(128)S(1)}, u32[]{:S(2)}, u32[]{:S(2)}) collective-permute-start(f32[4]{0:T(128)S(1)} %get-tuple-element.22), channel_id=1, source_target_pairs={{8,0},{16,8},{24,16},{32,24},{40,32},{48,40},{56,48},{64,56},{72,6... | collective-permute-start | bytes 56 | tf_op jit(solution)/shard_map/ppermute | solution.py:19
  155.7 5.8 %collective-permute-start.8 = (f32[4]{0:T(128)S(1)}, f32[4]{0:T(128)S(1)}, u32[]{:S(2)}, u32[]{:S(2)}) collective-permute-start(f32[4]{0:T(128)S(1)} %get-tuple-element.24), channel_id=1, source_target_pairs={{16,0},{24,8},{32,16},{40,24},{48,32},{56,40},{64,48},{72,56},{80,... | collective-permute-start | bytes 56 | tf_op jit(solution)/shard_map/ppermute | solution.py:19
where the time goes:
time: 261 us
  blocking collectives  94.5 us (36%)
  waiting for transfers between devices  74.7 us (29%)
  local copies, waits for them, and re-layouts  26 us (10%)
  matrix products  23.7 us (9%)
  starting transfers between devices  22.2 us (9%)
  other arithmetic  15 us (6%)
  between operations  4.49 us (2%)
    psum x1, blocking collectives, body(): lax.psum((jnp.sum(new_weight * local_energy), jnp.sum(new_weight)), ('ham...  78.8 us
    ppermute x9, waiting for transfers between devices, from_behind(): return lax.ppermute(block, axis, route)  74.7 us
    dot_general x4, matrix products, stop_terms(): jnp.einsum('vik,bkj->bvij', slab, theta, preferred_element_type=jnp.float32)  23.7 us
    ppermute x9, starting transfers between devices, from_behind(): return lax.ppermute(block, axis, route)  22.2 us
    dot_general x4, local copies, waits for them, and re-layouts, stop_terms(): jnp.einsum('vik,bkj->bvij', slab, theta, preferred_element_type=jnp.float32)  21 us
    unnamed x1, blocking collectives  15.7 us
    reduce_sum x1, other arithmetic, stop_terms(): exchange_part = jnp.sum(prod * jnp.swapaxes(prod, 2, 3), axis=(1, 2, 3))  12.3 us
  transfers between devices with their start and end apart: 9, of which 1 were waited for; matrix products, arithmetic and copies ran while one was open for 13% of the time, Pallas kernels for 0%

commit v1 on v0

v1 whole, which is shorter than its diff:
```python
import jax
import jax.numpy as jnp
from jax import lax
from jax.experimental import pallas as pl
from jax.experimental.pallas import tpu as pltpu
from jax.sharding import PartitionSpec as P

ORB = 1024
NOCC = 256
VECS = 4
STOPS = 4
WALKERS_DEV = 4
QUARTER = NOCC // 4
EIGHTH = NOCC // 8
FIELD_COUPLING = 0.02
DRIFT_COST = 0.0002
ONE_BODY = 1.0
MESH = pl.DeviceIdType.MESH
LANES = 128
EXCH_LANE = 16
WEIGHT_LANE = 17
LIVE_LANE = 18


def product_terms(prod):
    a, b = prod[:128, :128], prod[:128, 128:]
    c, d = prod[128:, :128], prod[128:, 128:]
    i = lax.broadcasted_iota(jnp.int32, (128, 128), 0)
    j = lax.broadcasted_iota(jnp.int32, (128, 128), 1)
    low = jnp.where(i >= j, a, d)
    high = jnp.where(i < j, a, d)
    pairs = high * low.T + b * c.T
    gap = jnp.where(i == j, a - d, 0.0)
    diag = jnp.where(i == j, a + d, 0.0)
    exchange = jnp.sum((pairs + pairs + gap * gap).reshape(16, 8, 128), axis=0)
    trace = jnp.sum(diag, axis=0, keepdims=True)
    return trace, exchange


def kernel(
    chol, green, fields, weights, partner, counts, out,
    slab, theta, far, transit, trace, exch, meta, meta_in, bias, bias_in, plane, line,
    load_sem, theta_sem, meta_sem, bias_sem, entry_send, entry_recv, transit_send, transit_recv,
    share_send, share_recv, direct_send, direct_recv, plane_sem, line_sem,
):
    h, g = lax.axis_index("ham"), lax.axis_index("walk")
    z, y_hi, core = h // 4, lax.rem(h // 2, 2), lax.rem(h, 2)
    x, y_lo = g // 2, lax.rem(g, 2)
    y = y_hi * 2 + y_lo

    def device(x=x, y_hi=y_hi, y_lo=y_lo, z=z, core=core):
        return {"ham": z * 4 + y_hi * 2 + core, "walk": x * 2 + y_lo}

    sibling = device(core=1 - core)
    cross = device(y_hi=1 - y_hi, y_lo=1 - y_lo)
    twin = device(y_lo=1 - y_lo)
    x_up, x_down = device(x=lax.rem(x + 1, 4)), device(x=lax.rem(x + 3, 4))
    z_down = device(z=lax.rem(z + 7, 8))
    z_on = device(z=lax.rem(z + 9 - 2 * y_hi, 8))
    sharers = (x_down, x_up, twin)
    color = lax.rem(x + 2 * y_lo, 4)
    cross_color = lax.rem(x + 2 * (1 - y_lo), 4)
    colors = (lax.rem(color + 1, 4), lax.rem(color + 3, 4), lax.rem(color + 2, 4))

    def plane_peer(d):
        yy = lax.rem(y + d // 4, 4)
        return device(x=lax.rem(x + d % 4, 4), y_hi=yy // 2, y_lo=lax.rem(yy, 2))

    def line_peer(d):
        return device(z=lax.rem(z + d, 8))

    def quarter(k):
        return pl.ds(pl.multiple_of(k * QUARTER, QUARTER), QUARTER)

    def first(k):
        return pl.ds(pl.multiple_of(k * QUARTER, EIGHTH), EIGHTH)

    def second(k):
        return pl.ds(pl.multiple_of(k * QUARTER + EIGHTH, EIGHTH), EIGHTH)

    def remote(src, dst, send, recv, to):
        return pltpu.make_async_remote_copy(src, dst, send, recv, device_id=to, device_id_type=MESH)

    barrier = pltpu.get_barrier_semaphore()
    pl.semaphore_signal(barrier, inc=1, device_id=sibling, device_id_type=MESH)
    for d in range(1, 16):
        pl.semaphore_signal(barrier, inc=1, device_id=plane_peer(d), device_id_type=MESH)
    for d in range(1, 8):
        pl.semaphore_signal(barrier, inc=1, device_id=line_peer(d), device_id_type=MESH)

    own_rows = pl.ds(core * WALKERS_DEV, WALKERS_DEV)
    load_slab = pltpu.make_async_copy(chol, slab, load_sem.at[0])
    load_theta = pltpu.make_async_copy(green, theta.at[own_rows], load_sem.at[1])
    load_slab.start()
    load_theta.start()
    row = lax.broadcasted_iota(jnp.int32, (8, LANES), 0)
    lane = lax.broadcasted_iota(jnp.int32, (8, LANES), 1)
    mine = row // 4 == core
    meta[...] = jnp.zeros_like(meta)
    meta[0:4, 0:16] = fields[...]
    meta[4:8, 0:16] = fields[...]
    values = meta[...]
    for i in range(WALKERS_DEV):
        values = jnp.where((row % 4 == i) & (lane == WEIGHT_LANE), weights[i], values)
    values = jnp.where((row % 4 < counts[0, 0]) & (lane == LIVE_LANE), 1.0, values)
    meta[...] = jnp.where(mine, values, 0.0)
    exch[...] = jnp.zeros_like(exch)

    pl.semaphore_wait(barrier, 23)

    swap_theta = remote(green, theta.at[own_rows], theta_sem.at[0], theta_sem.at[1], sibling)
    swap_meta = remote(meta, meta_in, meta_sem.at[0], meta_sem.at[1], sibling)

    def entry_out(src, v):
        return remote(src, far.at[0, v, quarter(cross_color)], entry_send.at[0, v], entry_recv.at[0, v], cross)

    def entry_in(s, v):
        rows = far.at[s, v, quarter(color)]
        return remote(rows, rows, entry_send.at[s, v], entry_recv.at[s, v], cross)

    def entry_on(v):
        rows = far.at[0, v, quarter(color)]
        return remote(rows, far.at[1, v, quarter(color)], entry_send.at[1, v], entry_recv.at[1, v], z_on)

    def transit_copy(v):
        return remote(chol.at[v, quarter(cross_color)], transit.at[v], transit_send.at[v], transit_recv.at[v], z_down)

    def part(s, k):
        return quarter(k) if s == 0 else first(k)

    def share_out(s, v, n):
        rows = far.at[s, v, part(s, color)]
        return remote(rows, rows, share_send.at[s, v, n], share_recv.at[s, v, n], sharers[n])

    def share_in(s, v, n):
        rows = far.at[s, v, part(s, colors[n])]
        return remote(rows, rows, share_send.at[s, v, n], share_recv.at[s, v, n], sharers[n])

    def direct(v, n):
        rows = second(colors[n])
        return remote(far.at[0, v, rows], far.at[1, v, rows], direct_send.at[v, n], direct_recv.at[v, n], z_on)

    def note(slot, w, terms):
        trace[slot, pl.ds(w, 1), :] = terms[0]
        exch[w] += terms[1]

    def own_step(w):
        prod = jnp.dot(slab[...].reshape(VECS * NOCC, ORB), theta[w], preferred_element_type=jnp.float32)
        for v in range(VECS):
            note(v, w, product_terms(prod[v * NOCC:(v + 1) * NOCC]))

    def far_step(s, v, base, count):
        vector = far[s, v]
        for n in range(count):
            w = base + n
            prod = jnp.dot(vector, theta[w], preferred_element_type=jnp.float32)
            note(VECS + v, w, product_terms(prod))

    def own_pair(v, n):
        base = jnp.where(v < 2, core, 1 - core) * WALKERS_DEV + lax.rem(v, 2) * 2
        own_step(base + n)

    @pl.when(core == 0)
    def _():
        @pl.when(y_hi == 0)
        def _():
            for v in range(VECS):
                transit_copy(v).start()

        @pl.when(y_hi == 1)
        def _():
            for v in range(VECS):
                entry_out(chol.at[v, quarter(cross_color)], v).start()

        swap_theta.start()
        swap_meta.start()
        load_slab.wait()
        load_theta.wait()

        def round_(v, carry):
            @pl.when(y_hi == 0)
            def _():
                transit_copy(v).wait_recv()
                entry_out(transit.at[v], v).start()

            own_pair(v, 0)
            entry_in(0, v).wait_recv()
            for n in range(3):
                share_out(0, v, n).start()

            @pl.when(v == 1)
            def _():
                swap_theta.wait_recv()

            own_pair(v, 1)

            @pl.when(v > 0)
            def _():
                for n in range(3):
                    share_in(0, v - 1, n).wait_recv()
                far_step(0, v - 1, 0, 8)

            return carry

        lax.fori_loop(0, VECS, round_, 0)
        for n in range(3):
            share_in(0, VECS - 1, n).wait_recv()
        far_step(0, VECS - 1, 0, 8)

    @pl.when(core == 1)
    def _():
        for v in range(VECS):
            entry_out(chol.at[v, quarter(cross_color)], v).start()
        swap_theta.start()
        swap_meta.start()
        load_slab.wait()
        load_theta.wait()
        near_base = (1 - y_hi) * WALKERS_DEV
        next_base = y_hi * WALKERS_DEV

        def finish(v):
            for n in range(3):
                share_in(1, v, n).wait_recv()
                direct(v, n).wait_recv()
            far_step(1, v, next_base, 4)

        def round_(v, carry):
            own_pair(v, 0)
            entry_in(0, v).wait_recv()
            for n in range(3):
                share_out(0, v, n).start()
            entry_on(v).start()

            own_pair(v, 1)

            @pl.when(v == 0)
            def _():
                swap_theta.wait_recv()

            for n in range(3):
                share_in(0, v, n).wait_recv()
                direct(v, n).start()
            entry_in(1, v).wait_recv()
            for n in range(3):
                share_out(1, v, n).start()
            far_step(0, v, near_base, 4)

            @pl.when(v > 0)
            def _():
                finish(v - 1)

            return carry

        lax.fori_loop(0, VECS, round_, 0)
        finish(VECS - 1)

    lower = row < 4
    tile = jnp.zeros((8, LANES), jnp.float32)
    own_cols = jnp.where(lower, 4 + 4 * core, 4 * core)
    far_cols = jnp.where(lower, 12 - 12 * core, 8 + 4 * core)
    for slot in range(2 * VECS):
        cols = own_cols if slot < VECS else far_cols
        total = jnp.sum(trace[slot], axis=1, keepdims=True)
        tile = jnp.where(lane == cols + slot % VECS, total, tile)
    exch_rows = jnp.sum(exch[...], axis=1)
    tile = jnp.where(lane == EXCH_LANE, jnp.sum(exch_rows, axis=1, keepdims=True), tile)
    bias[...] = tile
    swap_bias = remote(bias, bias_in, bias_sem.at[0], bias_sem.at[1], sibling)
    swap_bias.start()
    swap_meta.wait_recv()
    known = meta[...] + meta_in[...]
    swap_bias.wait_recv()
    full = bias[...] + bias_in[...]
    is_bias = lane < STOPS * VECS

    def pick(keep, values):
        return jnp.sum(jnp.where(keep, values, 0.0), axis=1, keepdims=True)

    squares = pick(is_bias, full * full)
    drift = pick(is_bias, full * known)
    exchange = pick(lane == EXCH_LANE, full)
    energy = ONE_BODY + (0.5 * squares - 0.5 * exchange) / (NOCC * STOPS * VECS)
    weight = pick(lane == WEIGHT_LANE, known) * pick(lane == LIVE_LANE, known)
    weight = weight * jnp.exp(FIELD_COUPLING * drift - DRIFT_COST * squares)
    here = jnp.where(lane == 0, weight, jnp.where(lane == 1, weight * energy, 0.0))

    my_plane = x * 4 + y
    plane[my_plane] = here
    for d in range(1, 16):
        remote(plane.at[my_plane], plane.at[my_plane], plane_sem.at[0], plane_sem.at[1], plane_peer(d)).start()
    some = plane.at[pl.ds(0, 15)]
    remote(some, some, plane_sem.at[0], plane_sem.at[1], sibling).wait_recv()
    summed = plane[0]
    for n in range(1, 16):
        summed = summed + plane[n]
    line[z] = summed
    for d in range(1, 8):
        remote(line.at[z], line.at[z], line_sem.at[0], line_sem.at[1], line_peer(d)).start()

    table = jnp.zeros((8, LANES), jnp.float32)
    for n in range(8):
        column = plane[(n // 2) * 4 + y_hi * 2 + n % 2]
        table = jnp.where(lane == n, pick(lane == 0, column), table)
    mate = jnp.zeros((8, LANES), jnp.float32)
    for i in range(WALKERS_DEV):
        found = (row == core * 4 + (partner[i] & 3)) & (lane == partner[i] // (WALKERS_DEV * 32))
        value = jnp.sum(pick(found, table), axis=0, keepdims=True)
        mate = jnp.where(row % 4 == i, value, mate)
    paired = 0.5 * (weight + mate)

    some_line = line.at[pl.ds(0, 7)]
    remote(some_line, some_line, line_sem.at[0], line_sem.at[1], sibling).wait_recv()
    summed = line[0]
    for n in range(1, 8):
        summed = summed + line[n]
    totals = jnp.sum(summed, axis=0, keepdims=True)
    top = jnp.broadcast_to(totals, (8, LANES))
    mean = pick(lane == 1, top) / pick(lane == 0, top)
    result = jnp.where(is_bias, full, 0.0)
    result = jnp.where(lane == 16, paired, result)
    result = jnp.where(lane == 17, energy, result)
    result = jnp.where(lane == 18, mean, result)
    out[...] = jnp.where(core == 0, result[0:4], result[4:8])

    remote(some, some, plane_sem.at[0], plane_sem.at[1], sibling).wait_send()
    remote(some_line, some_line, line_sem.at[0], line_sem.at[1], sibling).wait_send()
    swap_bias.wait_send()
    swap_theta.wait_send()
    swap_meta.wait_send()

    def sent(v, carry):
        for n in range(3):
            share_out(0, v, n).wait_send()

        @pl.when(core == 0)
        def _():
            @pl.when(y_hi == 0)
            def _():
                transit_copy(v).wait_send()

        entry_out(transit.at[v], v).wait_send()

        @pl.when(core == 1)
        def _():
            entry_on(v).wait_send()
            for n in range(3):
                share_out(1, v, n).wait_send()
                direct(v, n).wait_send()

        return carry

    lax.fori_loop(0, VECS, sent, 0)


def body(chol, green, fields, weights_in, partner, counts):
    anywhere = pl.BlockSpec(memory_space=pl.ANY)
    vmem = pl.BlockSpec(memory_space=pltpu.VMEM)
    smem = pl.BlockSpec(memory_space=pltpu.SMEM)
    dma = pltpu.SemaphoreType.DMA
    tile = pltpu.VMEM((8, LANES), jnp.float32)
    out = pl.pallas_call(
        kernel,
        out_shape=jax.ShapeDtypeStruct((4, LANES), jnp.float32),
        in_specs=[anywhere, anywhere, vmem, smem, smem, smem],
        out_specs=vmem,
        scratch_shapes=[
            pltpu.VMEM((VECS, NOCC, ORB), jnp.bfloat16),
            pltpu.VMEM((2 * WALKERS_DEV, ORB, NOCC), jnp.bfloat16),
            pltpu.VMEM((2, VECS, NOCC, ORB), jnp.bfloat16),
            pltpu.VMEM((VECS, QUARTER, ORB), jnp.bfloat16),
            pltpu.VMEM((2 * VECS, 8, LANES), jnp.float32),
            pltpu.VMEM((8, 8, LANES), jnp.float32),
            tile, tile, tile, tile,
            pltpu.VMEM((16, 8, LANES), jnp.float32),
            pltpu.VMEM((8, 8, LANES), jnp.float32),
            dma((2,)), dma((2,)), dma((2,)), dma((2,)),
            dma((2, VECS)), dma((2, VECS)), dma((VECS,)), dma((VECS,)),
            dma((2, VECS, 3)), dma((2, VECS, 3)), dma((VECS, 3)), dma((VECS, 3)),
            dma((2,)), dma((2,)),
        ],
        compiler_params=pltpu.CompilerParams(
            collective_id=0, has_side_effects=True, vmem_limit_bytes=48 * 2**20
        ),
        name="walkers",
    )(chol, green, fields, weights_in, partner, counts)
    return out[:, 16], out[:, 17], out[:, : STOPS * VECS], out[0, 18]


def solution(mesh):
    placed = (
        P("ham", None, None),
        P(("walk", "ham"), None, None),
        P(("walk", "ham"), None),
        P(("walk", "ham")),
        P(("walk", "ham")),
        P("walk", "ham"),
    )
    return jax.shard_map(
        body,
        mesh=mesh,
        in_specs=placed,
        out_specs=(P(("walk", "ham")), P(("walk", "ham")), P(("walk", "ham"), None), P()),
        check_vma=False,
    )
```

time: 261 us -> 63.9 us (0.24)
  blocking collectives: 94.5 us -> 0 us
  waiting for transfers between devices: 74.7 us -> 0 us
  Pallas kernels: 0 us -> 54.5 us
  matrix products: 23.7 us -> 0 us
  starting transfers between devices: 22.2 us -> 0 us
  local copies, waits for them, and re-layouts: 26 us -> 7.05 us
  other arithmetic: 15 us -> 0 us
  between operations: 4.49 us -> 1.3 us
    psum x1 -> x0, blocking collectives: 78.8 us -> none  [body(): lax.psum((jnp.sum(new_weight * local_energy), jnp.sum(new_weight)), ('ham...]
    ppermute x9 -> x0, waiting for transfers between devices: 74.7 us -> none  [from_behind(): return lax.ppermute(block, axis, route)]
    pallas_call x0 -> x1, Pallas kernels: none -> 54.5 us  [body(): pl.pallas_call(kernel, out_shape=jax.ShapeDtypeStruct((4, LANES), jnp.flo...]
    dot_general x4 -> x0, matrix products: 23.7 us -> none  [stop_terms(): jnp.einsum('vik,bkj->bvij', slab, theta, preferred_element_type=jnp.float32)]
    ppermute x9 -> x0, starting transfers between devices: 22.2 us -> none  [from_behind(): return lax.ppermute(block, axis, route)]
    dot_general x4 -> x0, local copies, waits for them, and re-layouts: 21 us -> none  [stop_terms(): jnp.einsum('vik,bkj->bvij', slab, theta, preferred_element_type=jnp.float32)]
    unnamed x1 -> x0, blocking collectives: 15.7 us -> none
    reduce_sum x4 -> x0, other arithmetic: 14.5 us -> none  [the longest x1 12.3 us: stop_terms(): exchange_part = jnp.sum(prod * jnp.swapaxes(prod, 2, 3), axis=(1, 2, 3))]
  transfers between devices with their start and end apart: 9 -> 0, of which waited for: 1 -> 0; matrix products, arithmetic and copies ran while one was open for 13% -> 0% of each run, Pallas kernels for 0% -> 0%
where the time goes in v1:
time: 63.9 us; the launch traced here: 62.9 us
  Pallas kernels  54.5 us (85%)
  local copies, waits for them, and re-layouts  7.05 us (11%)
  between operations  1.3 us (2%)
    pallas_call x1, Pallas kernels, body(): pl.pallas_call(kernel, out_shape=jax.ShapeDtypeStruct((4, LANES), jnp.flo...  54.5 us
    unnamed x11, local copies, waits for them, and re-layouts  5.74 us
    slice x2, local copies, waits for them, and re-layouts, body(): return (out[:, 16], out[:, 17], out[:, :STOPS * VECS], out[0, 18])  1.31 us

profile of v1, /device:TPU:1, one launch (start us, length us, event | category | flops | bytes accessed | tf_op | source)
XLA Modules:
  0.0 62.9 jit_solution(7626554807953274207)
XLA Ops:
  1.3 0.0 copy-start
  1.3 1.6 %copy-done = bf16[4,256,1024]{2,1,0:T(8,128)(2,1)S(1)} copy-done((bf16[4,256,1024]{2,1,0:T(8,128)(2,1)S(1)}, bf16[4,256,1024]{2,1,0:T(8,128)(2,1)}, u32[]{:S(2)}) %copy-start) | copy-done | bytes 2097176
  2.9 0.0 copy-start.1
  2.9 1.6 %copy-done.1 = bf16[4,1024,256]{2,1,0:T(8,128)(2,1)S(1)} copy-done((bf16[4,1024,256]{2,1,0:T(8,128)(2,1)S(1)}, bf16[4,1024,256]{2,1,0:T(8,128)(2,1)}, u32[]{:S(2)}) %copy-start.1) | copy-done | bytes 2097176
  4.5 0.0 copy-start.2
  4.5 0.7 %copy-done.2 = f32[4,16]{1,0:T(4,128)S(1)} copy-done((f32[4,16]{1,0:T(4,128)S(1)}, f32[4,16]{1,0:T(4,128)}, u32[]{:S(2)}) %copy-start.2) | copy-done | bytes 280
  5.1 0.0 copy-start.3
  5.1 0.7 %copy-done.3 = f32[4]{0:T(128)S(1)} copy-done((f32[4]{0:T(128)S(1)}, f32[4]{0:T(128)}, u32[]{:S(2)}) %copy-start.3) | copy-done | bytes 40
  5.8 0.0 copy-start.4
  5.8 0.7 %copy-done.4 = s32[4]{0:T(128)S(1)} copy-done((s32[4]{0:T(128)S(1)}, s32[4]{0:T(128)}, u32[]{:S(2)}) %copy-start.4) | copy-done | bytes 40
  6.5 54.5 %walkers.1 = f32[4,128]{1,0:T(4,128)S(1)} custom-call(bf16[4,256,1024]{2,1,0:T(8,128)(2,1)S(1)} %copy-done, bf16[4,1024,256]{2,1,0:T(8,128)(2,1)S(1)} %copy-done.1, f32[4,16]{1,0:T(4,128)S(1)} %copy-done.2, f32[4]{0:T(128)S(1)} %copy-done.3, s32[4]{0:T(128)S(1)} %copy-done.4, s32[1,1]{1,0:T(1,128)S(6)} %copy.11.counts), custom_call_target="tpu_custom_call" | custom-call | tf_op jit(solution)/shard_map/walkers/pallas_call | solution.py:361
  61.0 0.6 slice.15
  61.6 0.7 %slice_reduce_fusion = (f32[4]{0:T(128)}, f32[4]{0:T(128)}) fusion(f32[4,128]{1,0:T(4,128)S(1)} %walkers.1), kind=kLoop, calls=%fused_computation | loop fusion | bytes 64 | tf_op jit(solution)/shard_map/slice | solution.py:386
  62.3 0.6 copy.12
Async XLA Ops:
  1.3 1.6 %copy-start = (bf16[4,256,1024]{2,1,0:T(8,128)(2,1)S(1)}, bf16[4,256,1024]{2,1,0:T(8,128)(2,1)}, u32[]{:S(2)}) copy-start(bf16[4,256,1024]{2,1,0:T(8,128)(2,1)} %chol.1) | copy-start | bytes 6291460
  2.9 1.6 %copy-start.1 = (bf16[4,1024,256]{2,1,0:T(8,128)(2,1)S(1)}, bf16[4,1024,256]{2,1,0:T(8,128)(2,1)}, u32[]{:S(2)}) copy-start(bf16[4,1024,256]{2,1,0:T(8,128)(2,1)} %green.1) | copy-start | bytes 6291460
  4.5 0.7 %copy-start.2 = (f32[4,16]{1,0:T(4,128)S(1)}, f32[4,16]{1,0:T(4,128)}, u32[]{:S(2)}) copy-start(f32[4,16]{1,0:T(4,128)} %fields.1) | copy-start | bytes 772
  5.1 0.7 %copy-start.3 = (f32[4]{0:T(128)S(1)}, f32[4]{0:T(128)}, u32[]{:S(2)}) copy-start(f32[4]{0:T(128)} %weights.1) | copy-start | bytes 52
  5.8 0.7 %copy-start.4 = (s32[4]{0:T(128)S(1)}, s32[4]{0:T(128)}, u32[]{:S(2)}) copy-start(s32[4]{0:T(128)} %partner.1) | copy-start | bytes 52

commit v2 on v1

--- a/solution.py
+++ b/solution.py
@@ -20,6 +20,15 @@
 EXCH_LANE = 16
 WEIGHT_LANE = 17
 LIVE_LANE = 18
+PLAN_0 = (
+    "o0", "o1", "o2", "o3", "t0", "o4", "t1", "o5", "t2", "o6", "t3", "o7",
+    "e0", "e1", "e2", "s0", "a0", "e3", "s1", "a1", "s2", "a2", "s3", "a3",
+)
+PLAN_1 = (
+    "o0", "o1", "o2", "e0", "o3", "e1", "e2", "o4", "e3", "s0", "f0", "o5",
+    "s1", "f1", "p0", "s2", "f2", "o6", "s3", "f3", "o7", "g0", "q0", "p1",
+    "g1", "q1", "p2", "g2", "q2", "p3", "g3", "q3",
+)
 
 
 def product_terms(prod):
@@ -38,9 +47,9 @@
 
 
 def kernel(
-    chol, green, fields, weights, partner, counts, out,
-    slab, theta, far, transit, trace, exch, meta, meta_in, bias, bias_in, plane, line,
-    load_sem, theta_sem, meta_sem, bias_sem, entry_send, entry_recv, transit_send, transit_recv,
+    chol, green, fields_in, weights_in, partner_in, counts_in, out,
+    fields, weights, partner, counts, slab, theta, far, transit, trace, exch, meta, meta_in, bias, bias_in, plane, line,
+    small_sem, load_sem, theta_sem, meta_sem, bias_sem, entry_send, entry_recv, transit_send, transit_recv,
     share_send, share_recv, direct_send, direct_recv, plane_sem, line_sem,
 ):
     h, g = lax.axis_index("ham"), lax.axis_index("walk")
@@ -81,6 +90,20 @@
     def remote(src, dst, send, recv, to):
         return pltpu.make_async_remote_copy(src, dst, send, recv, device_id=to, device_id_type=MESH)
 
+    own_rows = pl.ds(core * WALKERS_DEV, WALKERS_DEV)
+    small = [
+        pltpu.make_async_copy(src, dst, small_sem.at[n])
+        for n, (src, dst) in enumerate(
+            ((fields_in, fields), (weights_in, weights), (partner_in, partner), (counts_in, counts))
+        )
+    ]
+    for copy in small:
+        copy.start()
+    load_slab = pltpu.make_async_copy(chol, slab, load_sem.at[0])
+    load_theta = pltpu.make_async_copy(green, theta.at[own_rows], load_sem.at[1])
+    load_slab.start()
+    load_theta.start()
+
     barrier = pltpu.get_barrier_semaphore()
     pl.semaphore_signal(barrier, inc=1, device_id=sibling, device_id_type=MESH)
     for d in range(1, 16):
@@ -88,11 +111,8 @@
     for d in range(1, 8):
         pl.semaphore_signal(barrier, inc=1, device_id=line_peer(d), device_id_type=MESH)
 
-    own_rows = pl.ds(core * WALKERS_DEV, WALKERS_DEV)
-    load_slab = pltpu.make_async_copy(chol, slab, load_sem.at[0])
-    load_theta = pltpu.make_async_copy(green, theta.at[own_rows], load_sem.at[1])
-    load_slab.start()
-    load_theta.start()
+    for copy in small:
+        copy.wait()
     row = lax.broadcasted_iota(jnp.int32, (8, LANES), 0)
     lane = lax.broadcasted_iota(jnp.int32, (8, LANES), 1)
     mine = row // 4 == core
@@ -106,9 +126,11 @@
     meta[...] = jnp.where(mine, values, 0.0)
     exch[...] = jnp.zeros_like(exch)
 
+    load_slab.wait()
+    load_theta.wait()
     pl.semaphore_wait(barrier, 23)
 
-    swap_theta = remote(green, theta.at[own_rows], theta_sem.at[0], theta_sem.at[1], sibling)
+    swap_theta = remote(theta.at[own_rows], theta.at[own_rows], theta_sem.at[0], theta_sem.at[1], sibling)
     swap_meta = remote(meta, meta_in, meta_sem.at[0], meta_sem.at[1], sibling)
 
     def entry_out(src, v):
@@ -123,7 +145,7 @@
         return remote(rows, far.at[1, v, quarter(color)], entry_send.at[1, v], entry_recv.at[1, v], z_on)
 
     def transit_copy(v):
-        return remote(chol.at[v, quarter(cross_color)], transit.at[v], transit_send.at[v], transit_recv.at[v], z_down)
+        return remote(slab.at[v, quarter(cross_color)], transit.at[v], transit_send.at[v], transit_recv.at[v], z_down)
 
     def part(s, k):
         return quarter(k) if s == 0 else first(k)
@@ -156,9 +178,63 @@
             prod = jnp.dot(vector, theta[w], preferred_element_type=jnp.float32)
             note(VECS + v, w, product_terms(prod))
 
-    def own_pair(v, n):
-        base = jnp.where(v < 2, core, 1 - core) * WALKERS_DEV + lax.rem(v, 2) * 2
-        own_step(base + n)
+    near_base = (1 - y_hi) * WALKERS_DEV
+    next_base = y_hi * WALKERS_DEV
+
+    def pass_on(v):
+        @pl.when(y_hi == 0)
+        def _():
+            transit_copy(v).wait_recv()
+            entry_out(transit.at[v], v).start()
+
+        @pl.when(y_hi == 1)
+        def _():
+            entry_out(slab.at[v, quarter(cross_color)], v).start()
+
+    def enter(v):
+        entry_in(0, v).wait_recv()
+        for n in range(3):
+            share_out(0, v, n).start()
+
+    def enter_on(v):
+        entry_in(0, v).wait_recv()
+        entry_on(v).start()
+        for n in range(3):
+            share_out(0, v, n).start()
+
+    def gather(v):
+        for n in range(3):
+            share_in(0, v, n).wait_recv()
+
+    def gather_on(v):
+        for n in range(3):
+            share_in(0, v, n).wait_recv()
+            direct(v, n).start()
+
+    def second_enter(v):
+        entry_in(1, v).wait_recv()
+        for n in range(3):
+            share_out(1, v, n).start()
+
+    def second_gather(v):
+        for n in range(3):
+            share_in(1, v, n).wait_recv()
+            direct(v, n).wait_recv()
+
+    def own(i):
+        if i == 4:
+            swap_theta.wait_recv()
+        base = core if i < 4 else 1 - core
+        own_step(base * WALKERS_DEV + i % 4)
+
+    def all_here(v):
+        far_step(0, v, 0, 2 * WALKERS_DEV)
+
+    def near_here(v):
+        far_step(0, v, near_base, WALKERS_DEV)
+
+    def next_here(v):
+        far_step(1, v, next_base, WALKERS_DEV)
 
     @pl.when(core == 0)
     def _():
@@ -167,92 +243,21 @@
             for v in range(VECS):
                 transit_copy(v).start()
 
-        @pl.when(y_hi == 1)
-        def _():
-            for v in range(VECS):
-                entry_out(chol.at[v, quarter(cross_color)], v).start()
-
         swap_theta.start()
         swap_meta.start()
-        load_slab.wait()
-        load_theta.wait()
-
-        def round_(v, carry):
-            @pl.when(y_hi == 0)
-            def _():
-                transit_copy(v).wait_recv()
-                entry_out(transit.at[v], v).start()
-
-            own_pair(v, 0)
-            entry_in(0, v).wait_recv()
-            for n in range(3):
-                share_out(0, v, n).start()
-
-            @pl.when(v == 1)
-            def _():
-                swap_theta.wait_recv()
-
-            own_pair(v, 1)
-
-            @pl.when(v > 0)
-            def _():
-                for n in range(3):
-                    share_in(0, v - 1, n).wait_recv()
-                far_step(0, v - 1, 0, 8)
-
-            return carry
-
-        lax.fori_loop(0, VECS, round_, 0)
-        for n in range(3):
-            share_in(0, VECS - 1, n).wait_recv()
-        far_step(0, VECS - 1, 0, 8)
+        steps = {"t": pass_on, "e": enter, "s": gather, "o": own, "a": all_here}
+        for step in PLAN_0:
+            steps[step[0]](int(step[1:]))
 
     @pl.when(core == 1)
     def _():
         for v in range(VECS):
-            entry_out(chol.at[v, quarter(cross_color)], v).start()
+            entry_out(slab.at[v, quarter(cross_color)], v).start()
         swap_theta.start()
         swap_meta.start()
-        load_slab.wait()
-        load_theta.wait()
-        near_base = (1 - y_hi) * WALKERS_DEV
-        next_base = y_hi * WALKERS_DEV
-
-        def finish(v):
-            for n in range(3):
-                share_in(1, v, n).wait_recv()
-                direct(v, n).wait_recv()
-            far_step(1, v, next_base, 4)
-
-        def round_(v, carry):
-            own_pair(v, 0)
-            entry_in(0, v).wait_recv()
-            for n in range(3):
-                share_out(0, v, n).start()
-            entry_on(v).start()
-
-            own_pair(v, 1)
-
-            @pl.when(v == 0)
-            def _():
-                swap_theta.wait_recv()
-
-            for n in range(3):
-                share_in(0, v, n).wait_recv()
-                direct(v, n).start()
-            entry_in(1, v).wait_recv()
-            for n in range(3):
-                share_out(1, v, n).start()
-            far_step(0, v, near_base, 4)
-
-            @pl.when(v > 0)
-            def _():
-                finish(v - 1)
-
-            return carry
-
-        lax.fori_loop(0, VECS, round_, 0)
-        finish(VECS - 1)
+        steps = {"e": enter_on, "s": gather_on, "f": second_enter, "g": second_gather, "o": own, "p": near_here, "q": next_here}
+        for step in PLAN_1:
+            steps[step[0]](int(step[1:]))
 
     lower = row < 4
     tile = jnp.zeros((8, LANES), jnp.float32)
@@ -355,15 +360,18 @@
 def body(chol, green, fields, weights_in, partner, counts):
     anywhere = pl.BlockSpec(memory_space=pl.ANY)
     vmem = pl.BlockSpec(memory_space=pltpu.VMEM)
-    smem = pl.BlockSpec(memory_space=pltpu.SMEM)
     dma = pltpu.SemaphoreType.DMA
     tile = pltpu.VMEM((8, LANES), jnp.float32)
     out = pl.pallas_call(
         kernel,
         out_shape=jax.ShapeDtypeStruct((4, LANES), jnp.float32),
-        in_specs=[anywhere, anywhere, vmem, smem, smem, smem],
+        in_specs=[anywhere] * 6,
         out_specs=vmem,
         scratch_shapes=[
+            pltpu.VMEM((WALKERS_DEV, STOPS * VECS), jnp.float32),
+            pltpu.SMEM((WALKERS_DEV,), jnp.float32),
+            pltpu.SMEM((WALKERS_DEV,), jnp.int32),
+            pltpu.SMEM((1, 1), jnp.int32),
             pltpu.VMEM((VECS, NOCC, ORB), jnp.bfloat16),
             pltpu.VMEM((2 * WALKERS_DEV, ORB, NOCC), jnp.bfloat16),
             pltpu.VMEM((2, VECS, NOCC, ORB), jnp.bfloat16),
@@ -373,13 +381,13 @@
             tile, tile, tile, tile,
             pltpu.VMEM((16, 8, LANES), jnp.float32),
             pltpu.VMEM((8, 8, LANES), jnp.float32),
-            dma((2,)), dma((2,)), dma((2,)), dma((2,)),
+            dma((4,)), dma((2,)), dma((2,)), dma((2,)), dma((2,)),
             dma((2, VECS)), dma((2, VECS)), dma((VECS,)), dma((VECS,)),
             dma((2, VECS, 3)), dma((2, VECS, 3)), dma((VECS, 3)), dma((VECS, 3)),
             dma((2,)), dma((2,)),
         ],
         compiler_params=pltpu.CompilerParams(
-            collective_id=0, has_side_effects=True, vmem_limit_bytes=48 * 2**20
+            collective_id=0, has_side_effects=True, vmem_limit_bytes=62 * 2**20
         ),
         name="walkers",
     )(chol, green, fields, weights_in, partner, counts)

time: 63.9 us -> 49.5 us (0.77); the launches traced: 62.9 us -> 49.4 us
  Pallas kernels: 54.5 us -> 44.1 us
  local copies, waits for them, and re-layouts: 7.05 us -> 4.01 us
    pallas_call x1, Pallas kernels: 54.5 us -> 44.1 us  [body(): pl.pallas_call(kernel, out_shape=jax.ShapeDtypeStruct((4, LANES), jnp.flo...]
    unnamed x11 -> x1, local copies, waits for them, and re-layouts: 5.74 us -> 1.26 us
    slice x2, local copies, waits for them, and re-layouts: 1.31 us -> 2.75 us  [body(): return (out[:, 16], out[:, 17], out[:, :STOPS * VECS], out[0, 18])]
where the time goes in v2:
time: 49.5 us; the launch traced here: 49.4 us
  Pallas kernels  44.1 us (89%)
  local copies, waits for them, and re-layouts  4.01 us (8%)
  between operations  1.29 us (3%)
    pallas_call x1, Pallas kernels, body(): pl.pallas_call(kernel, out_shape=jax.ShapeDtypeStruct((4, LANES), jnp.flo...  44.1 us
    slice x2, local copies, waits for them, and re-layouts, body(): return (out[:, 16], out[:, 17], out[:, :STOPS * VECS], out[0, 18])  2.75 us
    unnamed x1, local copies, waits for them, and re-layouts  1.26 us

profile of v2, /device:TPU:1, one launch (start us, length us, event | category | flops | bytes accessed | tf_op | source)
XLA Modules:
  0.0 49.4 jit_solution(11806150087251182071)
XLA Ops:
  1.3 44.1 %walkers.1 = f32[4,128]{1,0:T(4,128)} custom-call(bf16[4,256,1024]{2,1,0:T(8,128)(2,1)} %chol.1, bf16[4,1024,256]{2,1,0:T(8,128)(2,1)} %green.1, f32[4,16]{1,0:T(4,128)} %fields_in.1, f32[4]{0:T(128)} %weights_in.1, s32[4]{0:T(128)} %partner_in.1, s32[1,1]{1,0:T(1,128)S(6)} %copy.11.counts_in), custom_call_target="tpu_custom_call" | custom-call | tf_op jit(solution)/shard_map/walkers/pallas_call | solution.py:365
  45.3 1.3 %slice.15 = f32[1,1]{1,0:T(1,128)} slice(f32[4,128]{1,0:T(4,128)} %walkers.1), slice={[0:1], [18:19]} | slice | bytes 8 | tf_op jit(solution)/shard_map/slice | solution.py:394
  46.6 1.5 %slice_reduce_fusion = (f32[4]{0:T(128)}, f32[4]{0:T(128)}) fusion(f32[4,128]{1,0:T(4,128)} %walkers.1), kind=kLoop, calls=%fused_computation | loop fusion | bytes 64 | tf_op jit(solution)/shard_map/slice | solution.py:394
  48.1 1.3 %copy.12 = f32[4,16]{1,0:T(4,128)} copy(f32[4,16]{1,0:T(4,128)} %bitcast.2) | data formatting | bytes 512

commit v3 on v2

--- a/solution.py
+++ b/solution.py
@@ -1,3 +1,5 @@
+import functools
+
 import jax
 import jax.numpy as jnp
 from jax import lax
@@ -21,14 +23,30 @@
 WEIGHT_LANE = 17
 LIVE_LANE = 18
 PLAN_0 = (
-    "o0", "o1", "o2", "o3", "t0", "o4", "t1", "o5", "t2", "o6", "t3", "o7",
-    "e0", "e1", "e2", "s0", "a0", "e3", "s1", "a1", "s2", "a2", "s3", "a3",
+    "o0", "o1", "t0", "o2", "t1", "o3", "t2", "w0", "m0", "t3", "e0", "m1",
+    "e1", "m2", "e2", "s0", "a0", "e3", "b0", "s1", "a1", "b1", "m3", "s2",
+    "a2", "b2", "s3", "a3", "b3",
 )
 PLAN_1 = (
-    "o0", "o1", "o2", "e0", "o3", "e1", "e2", "o4", "e3", "s0", "f0", "o5",
-    "s1", "f1", "p0", "s2", "f2", "o6", "s3", "f3", "o7", "g0", "q0", "p1",
-    "g1", "q1", "p2", "g2", "q2", "p3", "g3", "q3",
+    "o0", "o1", "o2", "o3", "e0", "w0", "m0", "e1", "m1", "e2", "f0", "s0",
+    "m2", "e3", "f1", "s1", "p0", "f2", "s2", "p1", "m3", "f3", "s3", "p2",
+    "g0", "q0", "p3", "g1", "q1", "g2", "q2", "g3", "q3",
 )
+
+
+def rounds_of(plan, kinds):
+    rounds, steps = [], {}
+    order = list(kinds)
+    for name in plan:
+        kind = name[0]
+        if kind in kinds:
+            assert kind not in steps and all(order.index(k) < order.index(kind) for k in steps), name
+            steps[kind] = int(name[1:])
+        else:
+            rounds.append((steps, name))
+            steps = {}
+    assert not steps
+    return rounds
 
 
 def product_terms(prod):
@@ -48,7 +66,7 @@
 
 def kernel(
     chol, green, fields_in, weights_in, partner_in, counts_in, out,
-    fields, weights, partner, counts, slab, theta, far, transit, trace, exch, meta, meta_in, bias, bias_in, plane, line,
+    fields, weights, partner, counts, vecs, theta, carry, transit, trace, exch, meta, meta_in, bias, bias_in, plane, line,
     small_sem, load_sem, theta_sem, meta_sem, bias_sem, entry_send, entry_recv, transit_send, transit_recv,
     share_send, share_recv, direct_send, direct_recv, plane_sem, line_sem,
 ):
@@ -99,7 +117,7 @@
     ]
     for copy in small:
         copy.start()
-    load_slab = pltpu.make_async_copy(chol, slab, load_sem.at[0])
+    load_slab = pltpu.make_async_copy(chol, vecs.at[0], load_sem.at[0])
     load_theta = pltpu.make_async_copy(green, theta.at[own_rows], load_sem.at[1])
     load_slab.start()
     load_theta.start()
@@ -134,50 +152,52 @@
     swap_meta = remote(meta, meta_in, meta_sem.at[0], meta_sem.at[1], sibling)
 
     def entry_out(src, v):
-        return remote(src, far.at[0, v, quarter(cross_color)], entry_send.at[0, v], entry_recv.at[0, v], cross)
+        return remote(src, vecs.at[1, v, quarter(cross_color)], entry_send.at[0, v], entry_recv.at[0, v], cross)
 
     def entry_in(s, v):
-        rows = far.at[s, v, quarter(color)]
+        rows = vecs.at[1 + s, v, quarter(color)]
         return remote(rows, rows, entry_send.at[s, v], entry_recv.at[s, v], cross)
 
     def entry_on(v):
-        rows = far.at[0, v, quarter(color)]
-        return remote(rows, far.at[1, v, quarter(color)], entry_send.at[1, v], entry_recv.at[1, v], z_on)
+        rows = vecs.at[1, v, quarter(color)]
+        return remote(rows, vecs.at[2, v, quarter(color)], entry_send.at[1, v], entry_recv.at[1, v], z_on)
 
     def transit_copy(v):
-        return remote(slab.at[v, quarter(cross_color)], transit.at[v], transit_send.at[v], transit_recv.at[v], z_down)
+        return remote(vecs.at[0, v, quarter(cross_color)], transit.at[v], transit_send.at[v], transit_recv.at[v], z_down)
 
     def part(s, k):
         return quarter(k) if s == 0 else first(k)
 
     def share_out(s, v, n):
-        rows = far.at[s, v, part(s, color)]
+        rows = vecs.at[1 + s, v, part(s, color)]
         return remote(rows, rows, share_send.at[s, v, n], share_recv.at[s, v, n], sharers[n])
 
     def share_in(s, v, n):
-        rows = far.at[s, v, part(s, colors[n])]
+        rows = vecs.at[1 + s, v, part(s, colors[n])]
         return remote(rows, rows, share_send.at[s, v, n], share_recv.at[s, v, n], sharers[n])
 
     def direct(v, n):
         rows = second(colors[n])
-        return remote(far.at[0, v, rows], far.at[1, v, rows], direct_send.at[v, n], direct_recv.at[v, n], z_on)
-
-    def note(slot, w, terms):
-        trace[slot, pl.ds(w, 1), :] = terms[0]
-        exch[w] += terms[1]
-
-    def own_step(w):
-        prod = jnp.dot(slab[...].reshape(VECS * NOCC, ORB), theta[w], preferred_element_type=jnp.float32)
-        for v in range(VECS):
-            note(v, w, product_terms(prod[v * NOCC:(v + 1) * NOCC]))
-
-    def far_step(s, v, base, count):
-        vector = far[s, v]
-        for n in range(count):
-            w = base + n
-            prod = jnp.dot(vector, theta[w], preferred_element_type=jnp.float32)
-            note(VECS + v, w, product_terms(prod))
-
+        return remote(vecs.at[1, v, rows], vecs.at[2, v, rows], direct_send.at[v, n], direct_recv.at[v, n], z_on)
+
+    def note(slot, w, prod):
+        diagonal, exchange = product_terms(prod)
+        trace[slot, pl.ds(w, 1), :] = diagonal
+        exch[w] += exchange
+
+    def unit(s, v, base, last_slot, last_w):
+        slot = jnp.where(s == 0, v, VECS + v)
+        vector = vecs[s, v]
+        note(last_slot, last_w, carry[...])
+        for n in range(WALKERS_DEV):
+            prod = jnp.dot(vector, theta[base + n], preferred_element_type=jnp.float32)
+            if n < WALKERS_DEV - 1:
+                note(slot, base + n, prod)
+            else:
+                carry[...] = prod
+        return slot, base + WALKERS_DEV - 1
+
+    mine_base, other_base = core * WALKERS_DEV, (1 - core) * WALKERS_DEV
     near_base = (1 - y_hi) * WALKERS_DEV
     next_base = y_hi * WALKERS_DEV
 
@@ -189,7 +209,7 @@
 
         @pl.when(y_hi == 1)
         def _():
-            entry_out(slab.at[v, quarter(cross_color)], v).start()
+            entry_out(vecs.at[0, v, quarter(cross_color)], v).start()
 
     def enter(v):
         entry_in(0, v).wait_recv()
@@ -221,20 +241,34 @@
             share_in(1, v, n).wait_recv()
             direct(v, n).wait_recv()
 
-    def own(i):
-        if i == 4:
-            swap_theta.wait_recv()
-        base = core if i < 4 else 1 - core
-        own_step(base * WALKERS_DEV + i % 4)
-
-    def all_here(v):
-        far_step(0, v, 0, 2 * WALKERS_DEV)
-
-    def near_here(v):
-        far_step(0, v, near_base, WALKERS_DEV)
-
-    def next_here(v):
-        far_step(1, v, next_base, WALKERS_DEV)
+    def swapped(v):
+        swap_theta.wait_recv()
+
+    def run(plan, steps, units):
+        rounds = rounds_of(plan, steps)
+
+        def round_(i, last):
+            for kind, action in steps.items():
+                at = [(n, r[0][kind]) for n, r in enumerate(rounds) if kind in r[0]]
+                if at:
+                    v = sum(jnp.where(i == n, step, 0) for n, step in at)
+                    hit = functools.reduce(jnp.logical_or, [i == n for n, _ in at])
+                    pl.when(hit)(functools.partial(action, v))
+
+            def pick(field):
+                return sum(jnp.where(i == n, units(r[1])[field], 0) for n, r in enumerate(rounds))
+
+            return unit(pick(0), pick(1), pick(2), *last)
+
+        slot, w = lax.fori_loop(0, len(rounds), round_, (jnp.int32(0), jnp.int32(0)))
+        note(slot, w, carry[...])
+
+    own_units = {"o": (0, mine_base), "m": (0, other_base)}
+
+    def unit_of(table):
+        return lambda name: (table[name[0]][0], int(name[1:]), table[name[0]][1])
+
+    carry[...] = jnp.zeros_like(carry)
 
     @pl.when(core == 0)
     def _():
@@ -245,19 +279,17 @@
 
         swap_theta.start()
         swap_meta.start()
-        steps = {"t": pass_on, "e": enter, "s": gather, "o": own, "a": all_here}
-        for step in PLAN_0:
-            steps[step[0]](int(step[1:]))
+        steps = {"t": pass_on, "e": enter, "s": gather, "w": swapped}
+        run(PLAN_0, steps, unit_of(own_units | {"a": (1, mine_base), "b": (1, other_base)}))
 
     @pl.when(core == 1)
     def _():
         for v in range(VECS):
-            entry_out(slab.at[v, quarter(cross_color)], v).start()
+            entry_out(vecs.at[0, v, quarter(cross_color)], v).start()
         swap_theta.start()
         swap_meta.start()
-        steps = {"e": enter_on, "s": gather_on, "f": second_enter, "g": second_gather, "o": own, "p": near_here, "q": next_here}
-        for step in PLAN_1:
-            steps[step[0]](int(step[1:]))
+        steps = {"e": enter_on, "f": second_enter, "s": gather_on, "g": second_gather, "w": swapped}
+        run(PLAN_1, steps, unit_of(own_units | {"p": (1, near_base), "q": (2, next_base)}))
 
     lower = row < 4
     tile = jnp.zeros((8, LANES), jnp.float32)
@@ -372,9 +404,9 @@
             pltpu.SMEM((WALKERS_DEV,), jnp.float32),
             pltpu.SMEM((WALKERS_DEV,), jnp.int32),
             pltpu.SMEM((1, 1), jnp.int32),
-            pltpu.VMEM((VECS, NOCC, ORB), jnp.bfloat16),
+            pltpu.VMEM((3, VECS, NOCC, ORB), jnp.bfloat16),
             pltpu.VMEM((2 * WALKERS_DEV, ORB, NOCC), jnp.bfloat16),
-            pltpu.VMEM((2, VECS, NOCC, ORB), jnp.bfloat16),
+            pltpu.VMEM((NOCC, NOCC), jnp.float32),
             pltpu.VMEM((VECS, QUARTER, ORB), jnp.bfloat16),
             pltpu.VMEM((2 * VECS, 8, LANES), jnp.float32),
             pltpu.VMEM((8, 8, LANES), jnp.float32),

time: 49.5 us -> 50.4 us (1.018)
  Pallas kernels: 44.1 us -> 44.9 us
    pallas_call x1, Pallas kernels: 44.1 us -> 44.9 us  [body(): pl.pallas_call(kernel, out_shape=jax.ShapeDtypeStruct((4, LANES), jnp.flo...]
where the time goes in v3:
time: 50.4 us; the launch traced here: 50.2 us
  Pallas kernels  44.9 us (89%)
  local copies, waits for them, and re-layouts  4.01 us (8%)
  between operations  1.29 us (3%)
    pallas_call x1, Pallas kernels, body(): pl.pallas_call(kernel, out_shape=jax.ShapeDtypeStruct((4, LANES), jnp.flo...  44.9 us
    slice x2, local copies, waits for them, and re-layouts, body(): return (out[:, 16], out[:, 17], out[:, :STOPS * VECS], out[0, 18])  2.75 us
    unnamed x1, local copies, waits for them, and re-layouts  1.26 us

profile of v3, /device:TPU:1, one launch (start us, length us, event | category | flops | bytes accessed | tf_op | source)
XLA Modules:
  0.0 50.2 jit_solution(9878018256353257179)
XLA Ops:
  1.3 44.9 %walkers.1 = f32[4,128]{1,0:T(4,128)} custom-call(bf16[4,256,1024]{2,1,0:T(8,128)(2,1)} %chol.1, bf16[4,1024,256]{2,1,0:T(8,128)(2,1)} %green.1, f32[4,16]{1,0:T(4,128)} %fields_in.1, f32[4]{0:T(128)} %weights_in.1, s32[4]{0:T(128)} %partner_in.1, s32[1,1]{1,0:T(1,128)S(6)} %copy.11.counts_in), custom_call_target="tpu_custom_call" | custom-call | tf_op jit(solution)/shard_map/walkers/pallas_call | solution.py:397
  46.2 1.3 %slice.15 = f32[1,1]{1,0:T(1,128)} slice(f32[4,128]{1,0:T(4,128)} %walkers.1), slice={[0:1], [18:19]} | slice | bytes 8 | tf_op jit(solution)/shard_map/slice | solution.py:426
  47.4 1.5 %slice_reduce_fusion = (f32[4]{0:T(128)}, f32[4]{0:T(128)}) fusion(f32[4,128]{1,0:T(4,128)} %walkers.1), kind=kLoop, calls=%fused_computation | loop fusion | bytes 64 | tf_op jit(solution)/shard_map/slice | solution.py:426
  48.9 1.3 %copy.12 = f32[4,16]{1,0:T(4,128)} copy(f32[4,16]{1,0:T(4,128)} %bitcast.2) | data formatting | bytes 512

commit v4 on v3

--- a/solution.py
+++ b/solution.py
@@ -23,14 +23,14 @@
 WEIGHT_LANE = 17
 LIVE_LANE = 18
 PLAN_0 = (
-    "o0", "o1", "t0", "o2", "t1", "o3", "t2", "w0", "m0", "t3", "e0", "m1",
-    "e1", "m2", "e2", "s0", "a0", "e3", "b0", "s1", "a1", "b1", "m3", "s2",
-    "a2", "b2", "s3", "a3", "b3",
+    "o0", "t0", "o1", "t1", "e0", "o2", "t2", "o3", "t3", "e1", "w0", "m0",
+    "m1", "m2", "e2", "m3", "s0", "a0", "e3", "b0", "s1", "a1", "b1", "s2",
+    "b2", "a2", "s3", "b3", "a3",
 )
 PLAN_1 = (
-    "o0", "o1", "o2", "o3", "e0", "w0", "m0", "e1", "m1", "e2", "f0", "s0",
-    "m2", "e3", "f1", "s1", "p0", "f2", "s2", "p1", "m3", "f3", "s3", "p2",
-    "g0", "q0", "p3", "g1", "q1", "g2", "q2", "g3", "q3",
+    "o0", "e0", "o1", "e1", "o2", "e2", "f0", "s0", "o3", "e3", "f1", "s1",
+    "w0", "p0", "m0", "p1", "f2", "s2", "p2", "g0", "q0", "m1", "s3", "p3",
+    "f3", "g1", "m2", "m3", "q1", "g2", "q2", "g3", "q3",
 )
 
 
@@ -65,10 +65,10 @@
 
 
 def kernel(
-    chol, green, fields_in, weights_in, partner_in, counts_in, out,
-    fields, weights, partner, counts, vecs, theta, carry, transit, trace, exch, meta, meta_in, bias, bias_in, plane, line,
+    chol, green, fields_in, weights_in, partner_in, counts, out,
+    fields, weights, partner, vecs, theta, carry, transit, trace, exch, meta, meta_in, bias, bias_in, plane, line,
     small_sem, load_sem, theta_sem, meta_sem, bias_sem, entry_send, entry_recv, transit_send, transit_recv,
-    share_send, share_recv, direct_send, direct_recv, plane_sem, line_sem,
+    share_send, share_recv, direct_send, direct_recv, plane_sem, line_sem, hail_sem,
 ):
     h, g = lax.axis_index("ham"), lax.axis_index("walk")
     z, y_hi, core = h // 4, lax.rem(h // 2, 2), lax.rem(h, 2)
@@ -112,7 +112,7 @@
     small = [
         pltpu.make_async_copy(src, dst, small_sem.at[n])
         for n, (src, dst) in enumerate(
-            ((fields_in, fields), (weights_in, weights), (partner_in, partner), (counts_in, counts))
+            ((fields_in, fields), (weights_in, weights), (partner_in, partner))
         )
     ]
     for copy in small:
@@ -122,12 +122,19 @@
     load_slab.start()
     load_theta.start()
 
+    def hail(n):
+        for peer in neighbours:
+            pl.semaphore_signal(hail_sem.at[n], inc=1, device_id=peer, device_id_type=MESH)
+
+    def heard(n):
+        pl.semaphore_wait(hail_sem.at[n], 6)
+        if n < 2:
+            hail(n + 1)
+
     barrier = pltpu.get_barrier_semaphore()
-    pl.semaphore_signal(barrier, inc=1, device_id=sibling, device_id_type=MESH)
-    for d in range(1, 16):
-        pl.semaphore_signal(barrier, inc=1, device_id=plane_peer(d), device_id_type=MESH)
-    for d in range(1, 8):
-        pl.semaphore_signal(barrier, inc=1, device_id=line_peer(d), device_id_type=MESH)
+    neighbours = (x_up, x_down, cross, twin, line_peer(1), line_peer(7))
+    for peer in (sibling, *neighbours):
+        pl.semaphore_signal(barrier, inc=1, device_id=peer, device_id_type=MESH)
 
     for copy in small:
         copy.wait()
@@ -144,11 +151,9 @@
     meta[...] = jnp.where(mine, values, 0.0)
     exch[...] = jnp.zeros_like(exch)
 
-    load_slab.wait()
-    load_theta.wait()
-    pl.semaphore_wait(barrier, 23)
-
-    swap_theta = remote(theta.at[own_rows], theta.at[own_rows], theta_sem.at[0], theta_sem.at[1], sibling)
+    pl.semaphore_wait(barrier, 7)
+
+    swap_theta = remote(green, theta.at[own_rows], theta_sem.at[0], theta_sem.at[1], sibling)
     swap_meta = remote(meta, meta_in, meta_sem.at[0], meta_sem.at[1], sibling)
 
     def entry_out(src, v):
@@ -163,7 +168,7 @@
         return remote(rows, vecs.at[2, v, quarter(color)], entry_send.at[1, v], entry_recv.at[1, v], z_on)
 
     def transit_copy(v):
-        return remote(vecs.at[0, v, quarter(cross_color)], transit.at[v], transit_send.at[v], transit_recv.at[v], z_down)
+        return remote(chol.at[v, quarter(cross_color)], transit.at[v], transit_send.at[v], transit_recv.at[v], z_down)
 
     def part(s, k):
         return quarter(k) if s == 0 else first(k)
@@ -209,7 +214,7 @@
 
         @pl.when(y_hi == 1)
         def _():
-            entry_out(vecs.at[0, v, quarter(cross_color)], v).start()
+            entry_out(chol.at[v, quarter(cross_color)], v).start()
 
     def enter(v):
         entry_in(0, v).wait_recv()
@@ -248,6 +253,9 @@
         rounds = rounds_of(plan, steps)
 
         def round_(i, last):
+            for n in range(3):
+                pl.when(i == 3 * n + 2)(functools.partial(heard, n))
+
             for kind, action in steps.items():
                 at = [(n, r[0][kind]) for n, r in enumerate(rounds) if kind in r[0]]
                 if at:
@@ -279,15 +287,21 @@
 
         swap_theta.start()
         swap_meta.start()
+        hail(0)
+        load_slab.wait()
+        load_theta.wait()
         steps = {"t": pass_on, "e": enter, "s": gather, "w": swapped}
         run(PLAN_0, steps, unit_of(own_units | {"a": (1, mine_base), "b": (1, other_base)}))
 
     @pl.when(core == 1)
     def _():
         for v in range(VECS):
-            entry_out(vecs.at[0, v, quarter(cross_color)], v).start()
+            entry_out(chol.at[v, quarter(cross_color)], v).start()
         swap_theta.start()
         swap_meta.start()
+        hail(0)
+        load_slab.wait()
+        load_theta.wait()
         steps = {"e": enter_on, "f": second_enter, "s": gather_on, "g": second_gather, "w": swapped}
         run(PLAN_1, steps, unit_of(own_units | {"p": (1, near_base), "q": (2, next_base)}))
 
@@ -353,11 +367,17 @@
     totals = jnp.sum(summed, axis=0, keepdims=True)
     top = jnp.broadcast_to(totals, (8, LANES))
     mean = pick(lane == 1, top) / pick(lane == 0, top)
-    result = jnp.where(is_bias, full, 0.0)
-    result = jnp.where(lane == 16, paired, result)
-    result = jnp.where(lane == 17, energy, result)
-    result = jnp.where(lane == 18, mean, result)
-    out[...] = jnp.where(core == 0, result[0:4], result[4:8])
+    eye = (row == lane) | (row == lane + 4)
+    keep = eye & mine
+
+    def along(values):
+        return jnp.sum(jnp.where(keep, values, 0.0), axis=0, keepdims=True)
+
+    biases = jnp.where(core == 0, full[0:4], full[4:8])
+    out[0:4, :] = jnp.where(is_bias[0:4], biases, 0.0)
+    out[4:5, :] = along(paired)
+    out[5:6, :] = along(energy)
+    out[6:7, :] = mean[0:1] + jnp.zeros((1, LANES), jnp.float32)
 
     remote(some, some, plane_sem.at[0], plane_sem.at[1], sibling).wait_send()
     remote(some_line, some_line, line_sem.at[0], line_sem.at[1], sibling).wait_send()
@@ -387,6 +407,13 @@
         return carry
 
     lax.fori_loop(0, VECS, sent, 0)
+
+
+def deal(tile, paired, energy, bias, mean):
+    bias[...] = tile[0:WALKERS_DEV, 0:STOPS * VECS]
+    paired[...] = tile[4, 0:WALKERS_DEV]
+    energy[...] = tile[5, 0:WALKERS_DEV]
+    mean[...] = tile[6, 0:1]
 
 
 def body(chol, green, fields, weights_in, partner, counts):
@@ -396,14 +423,13 @@
     tile = pltpu.VMEM((8, LANES), jnp.float32)
     out = pl.pallas_call(
         kernel,
-        out_shape=jax.ShapeDtypeStruct((4, LANES), jnp.float32),
-        in_specs=[anywhere] * 6,
+        out_shape=jax.ShapeDtypeStruct((8, LANES), jnp.float32),
+        in_specs=[anywhere] * 5 + [pl.BlockSpec(memory_space=pltpu.SMEM)],
         out_specs=vmem,
         scratch_shapes=[
             pltpu.VMEM((WALKERS_DEV, STOPS * VECS), jnp.float32),
             pltpu.SMEM((WALKERS_DEV,), jnp.float32),
             pltpu.SMEM((WALKERS_DEV,), jnp.int32),
-            pltpu.SMEM((1, 1), jnp.int32),
             pltpu.VMEM((3, VECS, NOCC, ORB), jnp.bfloat16),
             pltpu.VMEM((2 * WALKERS_DEV, ORB, NOCC), jnp.bfloat16),
             pltpu.VMEM((NOCC, NOCC), jnp.float32),
@@ -413,17 +439,29 @@
             tile, tile, tile, tile,
             pltpu.VMEM((16, 8, LANES), jnp.float32),
             pltpu.VMEM((8, 8, LANES), jnp.float32),
-            dma((4,)), dma((2,)), dma((2,)), dma((2,)), dma((2,)),
+            dma((3,)), dma((2,)), dma((2,)), dma((2,)), dma((2,)),
             dma((2, VECS)), dma((2, VECS)), dma((VECS,)), dma((VECS,)),
             dma((2, VECS, 3)), dma((2, VECS, 3)), dma((VECS, 3)), dma((VECS, 3)),
-            dma((2,)), dma((2,)),
+            dma((2,)), dma((2,)), pltpu.SemaphoreType.REGULAR((3,)),
         ],
         compiler_params=pltpu.CompilerParams(
             collective_id=0, has_side_effects=True, vmem_limit_bytes=62 * 2**20
         ),
         name="walkers",
     )(chol, green, fields, weights_in, partner, counts)
-    return out[:, 16], out[:, 17], out[:, : STOPS * VECS], out[0, 18]
+    results = pl.pallas_call(
+        deal,
+        out_shape=(
+            jax.ShapeDtypeStruct((WALKERS_DEV,), jnp.float32),
+            jax.ShapeDtypeStruct((WALKERS_DEV,), jnp.float32),
+            jax.ShapeDtypeStruct((WALKERS_DEV, STOPS * VECS), jnp.float32),
+            jax.ShapeDtypeStruct((1,), jnp.float32),
+        ),
+        in_specs=[vmem],
+        out_specs=(vmem,) * 4,
+        name="deal",
+    )(out)
+    return results[0], results[1], results[2], results[3].reshape(())
 
 
 def solution(mesh):

time: 50.4 us -> 45.8 us (0.909)
  local copies, waits for them, and re-layouts: 4.01 us -> 0 us
  Pallas kernels: 44.9 us -> 44.3 us
    slice x2 -> x0, local copies, waits for them, and re-layouts: 2.75 us -> none  [body(): return (out[:, 16], out[:, 17], out[:, :STOPS * VECS], out[0, 18])]
    unnamed x1 -> x0, local copies, waits for them, and re-layouts: 1.26 us -> none
    pallas_call x1 -> x2, Pallas kernels: 44.9 us -> 44.3 us  [the longest x1 43.1 us: body(): pl.pallas_call(kernel, out_shape=jax.ShapeDtypeStruct((8, LANES), jnp.flo...]
where the time goes in v4:
time: 45.8 us; the launch traced here: 45.6 us
  Pallas kernels  44.3 us (97%)
  between operations  1.29 us (3%)
    pallas_call x1, Pallas kernels, body(): pl.pallas_call(kernel, out_shape=jax.ShapeDtypeStruct((8, LANES), jnp.flo...  43.1 us
    pallas_call x1, Pallas kernels, body(): pl.pallas_call(deal, out_shape=(jax.ShapeDtypeStruct((WALKERS_DEV,), jnp....  1.26 us

profile of v4, /device:TPU:1, one launch (start us, length us, event | category | flops | bytes accessed | tf_op | source)
XLA Modules:
  0.0 45.6 jit_solution(110274517890401501)
XLA Ops:
  1.3 43.1 %walkers.1.tile = f32[8,128]{1,0:T(8,128)} custom-call(bf16[4,256,1024]{2,1,0:T(8,128)(2,1)} %chol.1, bf16[4,1024,256]{2,1,0:T(8,128)(2,1)} %green.1, f32[4,16]{1,0:T(4,128)} %fields_in.1, f32[4]{0:T(128)} %weights_in.1, s32[4]{0:T(128)} %partner_in.1, s32[1,1]{1,0:T(1,128)S(6)} %copy.10.counts), custom_call_target="tpu_custom_call" | custom-call | tf_op jit(solution)/shard_map/walkers/pallas_call | solution.py:424
  44.4 1.3 %deal.1 = (f32[4]{0:T(128)}, f32[4]{0:T(128)}, f32[4,16]{1,0:T(4,128)}, f32[1]{0:T(128)}) custom-call(f32[8,128]{1,0:T(8,128)} %walkers.1.tile), custom_call_target="tpu_custom_call" | custom-call | tf_op jit(solution)/shard_map/deal/pallas_call | solution.py:452

commit v5 on v4

--- a/solution.py
+++ b/solution.py
@@ -23,14 +23,14 @@
 WEIGHT_LANE = 17
 LIVE_LANE = 18
 PLAN_0 = (
-    "o0", "t0", "o1", "t1", "e0", "o2", "t2", "o3", "t3", "e1", "w0", "m0",
-    "m1", "m2", "e2", "m3", "s0", "a0", "e3", "b0", "s1", "a1", "b1", "s2",
-    "b2", "a2", "s3", "b3", "a3",
+    "o0", "t0", "o1", "t1", "o2", "t2", "u0", "w0", "m0", "t3", "u1", "m1",
+    "u2", "e0", "m2", "u3", "e1", "o3", "e2", "s0", "a0", "m3", "e3", "b0",
+    "s1", "a1", "b1", "s2", "a2", "b2", "s3", "a3", "b3",
 )
 PLAN_1 = (
-    "o0", "e0", "o1", "e1", "o2", "e2", "f0", "s0", "o3", "e3", "f1", "s1",
-    "w0", "p0", "m0", "p1", "f2", "s2", "p2", "g0", "q0", "m1", "s3", "p3",
-    "f3", "g1", "m2", "m3", "q1", "g2", "q2", "g3", "q3",
+    "o0", "e0", "o1", "o2", "e1", "o3", "e2", "f0", "s0", "w0", "m0", "m1",
+    "e3", "s1", "p0", "p1", "m2", "f1", "s2", "g0", "q0", "f2", "s3", "p2",
+    "f3", "p3", "g1", "q1", "m3", "g2", "q2", "g3", "q3",
 )
 
 
@@ -108,6 +108,20 @@
     def remote(src, dst, send, recv, to):
         return pltpu.make_async_remote_copy(src, dst, send, recv, device_id=to, device_id_type=MESH)
 
+    def hail(n):
+        for peer in neighbours:
+            pl.semaphore_signal(hail_sem.at[n], inc=1, device_id=peer, device_id_type=MESH)
+
+    def heard(n):
+        pl.semaphore_wait(hail_sem.at[n], 6)
+        if n < 2:
+            hail(n + 1)
+
+    barrier = pltpu.get_barrier_semaphore()
+    neighbours = (x_up, x_down, cross, twin, line_peer(1), line_peer(7))
+    for peer in (sibling, *neighbours):
+        pl.semaphore_signal(barrier, inc=1, device_id=peer, device_id_type=MESH)
+
     own_rows = pl.ds(core * WALKERS_DEV, WALKERS_DEV)
     small = [
         pltpu.make_async_copy(src, dst, small_sem.at[n])
@@ -122,68 +136,57 @@
     load_slab.start()
     load_theta.start()
 
-    def hail(n):
-        for peer in neighbours:
-            pl.semaphore_signal(hail_sem.at[n], inc=1, device_id=peer, device_id_type=MESH)
-
-    def heard(n):
-        pl.semaphore_wait(hail_sem.at[n], 6)
-        if n < 2:
-            hail(n + 1)
-
-    barrier = pltpu.get_barrier_semaphore()
-    neighbours = (x_up, x_down, cross, twin, line_peer(1), line_peer(7))
-    for peer in (sibling, *neighbours):
-        pl.semaphore_signal(barrier, inc=1, device_id=peer, device_id_type=MESH)
-
-    for copy in small:
-        copy.wait()
+    pl.semaphore_wait(barrier, 7)
+
+    swap_theta = remote(green, theta.at[own_rows], theta_sem.at[0], theta_sem.at[1], sibling)
+    swap_meta = remote(meta, meta_in, meta_sem.at[0], meta_sem.at[1], sibling)
+
+    def entry_out(src, v):
+        return remote(src, vecs.at[1, v, quarter(cross_color)], entry_send.at[0, v], entry_recv.at[0, v], cross)
+
+    def entry_in(s, v):
+        rows = vecs.at[1 + s, v, quarter(color)]
+        return remote(rows, rows, entry_send.at[s, v], entry_recv.at[s, v], cross)
+
+    def entry_on(v):
+        rows = vecs.at[1, v, quarter(color)]
+        return remote(rows, vecs.at[2, v, quarter(color)], entry_send.at[1, v], entry_recv.at[1, v], z_on)
+
+    def transit_copy(v):
+        return remote(chol.at[v, quarter(cross_color)], transit.at[v], transit_send.at[v], transit_recv.at[v], z_down)
+
+    def part(s, k):
+        return quarter(k) if s == 0 else first(k)
+
+    def share_out(s, v, n):
+        rows = vecs.at[1 + s, v, part(s, color)]
+        return remote(rows, rows, share_send.at[s, v, n], share_recv.at[s, v, n], sharers[n])
+
+    def share_in(s, v, n):
+        rows = vecs.at[1 + s, v, part(s, colors[n])]
+        return remote(rows, rows, share_send.at[s, v, n], share_recv.at[s, v, n], sharers[n])
+
+    def direct(v, n):
+        rows = second(colors[n])
+        return remote(vecs.at[1, v, rows], vecs.at[2, v, rows], direct_send.at[v, n], direct_recv.at[v, n], z_on)
+
     row = lax.broadcasted_iota(jnp.int32, (8, LANES), 0)
     lane = lax.broadcasted_iota(jnp.int32, (8, LANES), 1)
     mine = row // 4 == core
-    meta[...] = jnp.zeros_like(meta)
-    meta[0:4, 0:16] = fields[...]
-    meta[4:8, 0:16] = fields[...]
-    values = meta[...]
-    for i in range(WALKERS_DEV):
-        values = jnp.where((row % 4 == i) & (lane == WEIGHT_LANE), weights[i], values)
-    values = jnp.where((row % 4 < counts[0, 0]) & (lane == LIVE_LANE), 1.0, values)
-    meta[...] = jnp.where(mine, values, 0.0)
-    exch[...] = jnp.zeros_like(exch)
-
-    pl.semaphore_wait(barrier, 7)
-
-    swap_theta = remote(green, theta.at[own_rows], theta_sem.at[0], theta_sem.at[1], sibling)
-    swap_meta = remote(meta, meta_in, meta_sem.at[0], meta_sem.at[1], sibling)
-
-    def entry_out(src, v):
-        return remote(src, vecs.at[1, v, quarter(cross_color)], entry_send.at[0, v], entry_recv.at[0, v], cross)
-
-    def entry_in(s, v):
-        rows = vecs.at[1 + s, v, quarter(color)]
-        return remote(rows, rows, entry_send.at[s, v], entry_recv.at[s, v], cross)
-
-    def entry_on(v):
-        rows = vecs.at[1, v, quarter(color)]
-        return remote(rows, vecs.at[2, v, quarter(color)], entry_send.at[1, v], entry_recv.at[1, v], z_on)
-
-    def transit_copy(v):
-        return remote(chol.at[v, quarter(cross_color)], transit.at[v], transit_send.at[v], transit_recv.at[v], z_down)
-
-    def part(s, k):
-        return quarter(k) if s == 0 else first(k)
-
-    def share_out(s, v, n):
-        rows = vecs.at[1 + s, v, part(s, color)]
-        return remote(rows, rows, share_send.at[s, v, n], share_recv.at[s, v, n], sharers[n])
-
-    def share_in(s, v, n):
-        rows = vecs.at[1 + s, v, part(s, colors[n])]
-        return remote(rows, rows, share_send.at[s, v, n], share_recv.at[s, v, n], sharers[n])
-
-    def direct(v, n):
-        rows = second(colors[n])
-        return remote(vecs.at[1, v, rows], vecs.at[2, v, rows], direct_send.at[v, n], direct_recv.at[v, n], z_on)
+
+    def prepare():
+        for copy in small:
+            copy.wait()
+        meta[...] = jnp.zeros_like(meta)
+        meta[0:4, 0:16] = fields[...]
+        meta[4:8, 0:16] = fields[...]
+        values = meta[...]
+        for i in range(WALKERS_DEV):
+            values = jnp.where((row % 4 == i) & (lane == WEIGHT_LANE), weights[i], values)
+        values = jnp.where((row % 4 < counts[0, 0]) & (lane == LIVE_LANE), 1.0, values)
+        meta[...] = jnp.where(mine, values, 0.0)
+        exch[...] = jnp.zeros_like(exch)
+        swap_meta.start()
 
     def note(slot, w, prod):
         diagonal, exchange = product_terms(prod)
@@ -212,6 +215,7 @@
             transit_copy(v).wait_recv()
             entry_out(transit.at[v], v).start()
 
+    def send_on(v):
         @pl.when(y_hi == 1)
         def _():
             entry_out(chol.at[v, quarter(cross_color)], v).start()
@@ -286,11 +290,11 @@
                 transit_copy(v).start()
 
         swap_theta.start()
-        swap_meta.start()
         hail(0)
+        prepare()
         load_slab.wait()
         load_theta.wait()
-        steps = {"t": pass_on, "e": enter, "s": gather, "w": swapped}
+        steps = {"t": pass_on, "u": send_on, "e": enter, "s": gather, "w": swapped}
         run(PLAN_0, steps, unit_of(own_units | {"a": (1, mine_base), "b": (1, other_base)}))
 
     @pl.when(core == 1)
@@ -298,8 +302,8 @@
         for v in range(VECS):
             entry_out(chol.at[v, quarter(cross_color)], v).start()
         swap_theta.start()
-        swap_meta.start()
         hail(0)
+        prepare()
         load_slab.wait()
         load_theta.wait()
         steps = {"e": enter_on, "f": second_enter, "s": gather_on, "g": second_gather, "w": swapped}
@@ -337,7 +341,7 @@
 
     my_plane = x * 4 + y
     plane[my_plane] = here
-    for d in range(1, 16):
+    for d in (10, 9, 11, 6, 14, 5, 7, 13, 15, 2, 8, 1, 3, 4, 12):
         remote(plane.at[my_plane], plane.at[my_plane], plane_sem.at[0], plane_sem.at[1], plane_peer(d)).start()
     some = plane.at[pl.ds(0, 15)]
     remote(some, some, plane_sem.at[0], plane_sem.at[1], sibling).wait_recv()
@@ -345,7 +349,7 @@
     for n in range(1, 16):
         summed = summed + plane[n]
     line[z] = summed
-    for d in range(1, 8):
+    for d in (4, 3, 5, 2, 6, 1, 7):
         remote(line.at[z], line.at[z], line_sem.at[0], line_sem.at[1], line_peer(d)).start()
 
     table = jnp.zeros((8, LANES), jnp.float32)

time: 45.8 us -> 45.3 us (0.989)
    pallas_call x1, Pallas kernels: 43.1 us -> 42.6 us  [body(): pl.pallas_call(kernel, out_shape=jax.ShapeDtypeStruct((8, LANES), jnp.flo...]
where the time goes in v5:
time: 45.3 us; the launch traced here: 45.1 us
  Pallas kernels  43.9 us (97%)
  between operations  1.29 us (3%)
    pallas_call x1, Pallas kernels, body(): pl.pallas_call(kernel, out_shape=jax.ShapeDtypeStruct((8, LANES), jnp.flo...  42.6 us
    pallas_call x1, Pallas kernels, body(): pl.pallas_call(deal, out_shape=(jax.ShapeDtypeStruct((WALKERS_DEV,), jnp....  1.26 us

profile of v5, /device:TPU:1, one launch (start us, length us, event | category | flops | bytes accessed | tf_op | source)
XLA Modules:
  0.0 45.1 jit_solution(12531049643952263186)
XLA Ops:
  1.3 42.6 %walkers.1.tile = f32[8,128]{1,0:T(8,128)} custom-call(bf16[4,256,1024]{2,1,0:T(8,128)(2,1)} %chol.1, bf16[4,1024,256]{2,1,0:T(8,128)(2,1)} %green.1, f32[4,16]{1,0:T(4,128)} %fields_in.1, f32[4]{0:T(128)} %weights_in.1, s32[4]{0:T(128)} %partner_in.1, s32[1,1]{1,0:T(1,128)S(6)} %copy.10.counts), custom_call_target="tpu_custom_call" | custom-call | tf_op jit(solution)/shard_map/walkers/pallas_call | solution.py:428
  43.9 1.3 %deal.1 = (f32[4]{0:T(128)}, f32[4]{0:T(128)}, f32[4,16]{1,0:T(4,128)}, f32[1]{0:T(128)}) custom-call(f32[8,128]{1,0:T(8,128)} %walkers.1.tile), custom_call_target="tpu_custom_call" | custom-call | tf_op jit(solution)/shard_map/deal/pallas_call | solution.py:456

commit v6 on v5

--- a/solution.py
+++ b/solution.py
@@ -23,14 +23,14 @@
 WEIGHT_LANE = 17
 LIVE_LANE = 18
 PLAN_0 = (
-    "o0", "t0", "o1", "t1", "o2", "t2", "u0", "w0", "m0", "t3", "u1", "m1",
-    "u2", "e0", "m2", "u3", "e1", "o3", "e2", "s0", "a0", "m3", "e3", "b0",
+    "o0", "o1", "o2", "t0", "u0", "o3", "t1", "u1", "w0", "m0", "t2", "u2",
+    "m1", "t3", "u3", "e0", "m2", "e1", "m3", "e2", "s0", "a0", "e3", "b0",
     "s1", "a1", "b1", "s2", "a2", "b2", "s3", "a3", "b3",
 )
 PLAN_1 = (
-    "o0", "e0", "o1", "o2", "e1", "o3", "e2", "f0", "s0", "w0", "m0", "m1",
-    "e3", "s1", "p0", "p1", "m2", "f1", "s2", "g0", "q0", "f2", "s3", "p2",
-    "f3", "p3", "g1", "q1", "m3", "g2", "q2", "g3", "q3",
+    "o0", "e0", "o1", "e1", "o2", "e2", "f0", "o3", "e3", "f1", "s0", "w0",
+    "m0", "f2", "s1", "m1", "p0", "f3", "s2", "m2", "s3", "p1", "g0", "q0",
+    "p2", "g1", "q1", "p3", "g2", "q2", "m3", "g3", "q3",
 )
 
 
@@ -133,8 +133,6 @@
         copy.start()
     load_slab = pltpu.make_async_copy(chol, vecs.at[0], load_sem.at[0])
     load_theta = pltpu.make_async_copy(green, theta.at[own_rows], load_sem.at[1])
-    load_slab.start()
-    load_theta.start()
 
     pl.semaphore_wait(barrier, 7)
 
@@ -290,6 +288,8 @@
                 transit_copy(v).start()
 
         swap_theta.start()
+        load_slab.start()
+        load_theta.start()
         hail(0)
         prepare()
         load_slab.wait()
@@ -302,6 +302,8 @@
         for v in range(VECS):
             entry_out(chol.at[v, quarter(cross_color)], v).start()
         swap_theta.start()
+        load_slab.start()
+        load_theta.start()
         hail(0)
         prepare()
         load_slab.wait()
@@ -337,7 +339,8 @@
     energy = ONE_BODY + (0.5 * squares - 0.5 * exchange) / (NOCC * STOPS * VECS)
     weight = pick(lane == WEIGHT_LANE, known) * pick(lane == LIVE_LANE, known)
     weight = weight * jnp.exp(FIELD_COUPLING * drift - DRIFT_COST * squares)
-    here = jnp.where(lane == 0, weight, jnp.where(lane == 1, weight * energy, 0.0))
+    spread = jnp.where((row == lane) | (lane == 8), weight, jnp.where(lane == 9, weight * energy, 0.0))
+    here = jnp.sum(spread, axis=0, keepdims=True)
 
     my_plane = x * 4 + y
     plane[my_plane] = here
@@ -352,39 +355,7 @@
     for d in (4, 3, 5, 2, 6, 1, 7):
         remote(line.at[z], line.at[z], line_sem.at[0], line_sem.at[1], line_peer(d)).start()
 
-    table = jnp.zeros((8, LANES), jnp.float32)
-    for n in range(8):
-        column = plane[(n // 2) * 4 + y_hi * 2 + n % 2]
-        table = jnp.where(lane == n, pick(lane == 0, column), table)
-    mate = jnp.zeros((8, LANES), jnp.float32)
-    for i in range(WALKERS_DEV):
-        found = (row == core * 4 + (partner[i] & 3)) & (lane == partner[i] // (WALKERS_DEV * 32))
-        value = jnp.sum(pick(found, table), axis=0, keepdims=True)
-        mate = jnp.where(row % 4 == i, value, mate)
-    paired = 0.5 * (weight + mate)
-
-    some_line = line.at[pl.ds(0, 7)]
-    remote(some_line, some_line, line_sem.at[0], line_sem.at[1], sibling).wait_recv()
-    summed = line[0]
-    for n in range(1, 8):
-        summed = summed + line[n]
-    totals = jnp.sum(summed, axis=0, keepdims=True)
-    top = jnp.broadcast_to(totals, (8, LANES))
-    mean = pick(lane == 1, top) / pick(lane == 0, top)
-    eye = (row == lane) | (row == lane + 4)
-    keep = eye & mine
-
-    def along(values):
-        return jnp.sum(jnp.where(keep, values, 0.0), axis=0, keepdims=True)
-
-    biases = jnp.where(core == 0, full[0:4], full[4:8])
-    out[0:4, :] = jnp.where(is_bias[0:4], biases, 0.0)
-    out[4:5, :] = along(paired)
-    out[5:6, :] = along(energy)
-    out[6:7, :] = mean[0:1] + jnp.zeros((1, LANES), jnp.float32)
-
     remote(some, some, plane_sem.at[0], plane_sem.at[1], sibling).wait_send()
-    remote(some_line, some_line, line_sem.at[0], line_sem.at[1], sibling).wait_send()
     swap_bias.wait_send()
     swap_theta.wait_send()
     swap_meta.wait_send()
@@ -411,6 +382,37 @@
         return carry
 
     lax.fori_loop(0, VECS, sent, 0)
+
+    table = jnp.zeros((8, LANES), jnp.float32)
+    for n in range(8):
+        table = jnp.where(row == n, plane[(n // 2) * 4 + y_hi * 2 + n % 2], table)
+    mate = jnp.zeros((8, LANES), jnp.float32)
+    for i in range(WALKERS_DEV):
+        found = (row == partner[i] // (WALKERS_DEV * 32)) & (lane == core * 4 + (partner[i] & 3))
+        value = jnp.sum(pick(found, table), axis=0, keepdims=True)
+        mate = jnp.where(row % 4 == i, value, mate)
+    paired = 0.5 * (weight + mate)
+
+    some_line = line.at[pl.ds(0, 7)]
+    remote(some_line, some_line, line_sem.at[0], line_sem.at[1], sibling).wait_recv()
+    summed = line[0]
+    for n in range(1, 8):
+        summed = summed + line[n]
+    top = jnp.broadcast_to(summed, (8, LANES))
+    mean = pick(lane == 9, top) / pick(lane == 8, top)
+    eye = (row == lane) | (row == lane + 4)
+    keep = eye & mine
+
+    def along(values):
+        return jnp.sum(jnp.where(keep, values, 0.0), axis=0, keepdims=True)
+
+    biases = jnp.where(core == 0, full[0:4], full[4:8])
+    out[0:4, :] = jnp.where(is_bias[0:4], biases, 0.0)
+    out[4:5, :] = along(paired)
+    out[5:6, :] = along(energy)
+    out[6:7, :] = mean[0:1] + jnp.zeros((1, LANES), jnp.float32)
+
+    remote(some_line, some_line, line_sem.at[0], line_sem.at[1], sibling).wait_send()
 
 
 def deal(tile, paired, energy, bias, mean):
@@ -441,8 +443,8 @@
             pltpu.VMEM((2 * VECS, 8, LANES), jnp.float32),
             pltpu.VMEM((8, 8, LANES), jnp.float32),
             tile, tile, tile, tile,
-            pltpu.VMEM((16, 8, LANES), jnp.float32),
-            pltpu.VMEM((8, 8, LANES), jnp.float32),
+            pltpu.VMEM((16, 1, LANES), jnp.float32),
+            pltpu.VMEM((8, 1, LANES), jnp.float32),
             dma((3,)), dma((2,)), dma((2,)), dma((2,)), dma((2,)),
             dma((2, VECS)), dma((2, VECS)), dma((VECS,)), dma((VECS,)),
             dma((2, VECS, 3)), dma((2, VECS, 3)), dma((VECS, 3)), dma((VECS, 3)),

time: 45.3 us -> 45 us (level)
  no operation moved by 1% of the time
where the time goes in v6:
time: 45 us; the launch traced here: 44.9 us
  Pallas kernels  43.6 us (97%)
  between operations  1.29 us (3%)
    pallas_call x1, Pallas kernels, body(): pl.pallas_call(kernel, out_shape=jax.ShapeDtypeStruct((8, LANES), jnp.flo...  42.3 us
    pallas_call x1, Pallas kernels, body(): pl.pallas_call(deal, out_shape=(jax.ShapeDtypeStruct((WALKERS_DEV,), jnp....  1.26 us

profile of v6, /device:TPU:1, one launch (start us, length us, event | category | flops | bytes accessed | tf_op | source)
XLA Modules:
  0.0 44.9 jit_solution(9744105401829603718)
XLA Ops:
  1.3 42.3 %walkers.1.tile = f32[8,128]{1,0:T(8,128)} custom-call(bf16[4,256,1024]{2,1,0:T(8,128)(2,1)} %chol.1, bf16[4,1024,256]{2,1,0:T(8,128)(2,1)} %green.1, f32[4,16]{1,0:T(4,128)} %fields_in.1, f32[4]{0:T(128)} %weights_in.1, s32[4]{0:T(128)} %partner_in.1, s32[1,1]{1,0:T(1,128)S(6)} %copy.10.counts), custom_call_target="tpu_custom_call" | custom-call | tf_op jit(solution)/shard_map/walkers/pallas_call | solution.py:430
  43.6 1.3 %deal.1 = (f32[4]{0:T(128)}, f32[4]{0:T(128)}, f32[4,16]{1,0:T(4,128)}, f32[1]{0:T(128)}) custom-call(f32[8,128]{1,0:T(8,128)} %walkers.1.tile), custom_call_target="tpu_custom_call" | custom-call | tf_op jit(solution)/shard_map/deal/pallas_call | solution.py:458

commit v7 on v6

--- a/solution.py
+++ b/solution.py
@@ -136,7 +136,7 @@
 
     pl.semaphore_wait(barrier, 7)
 
-    swap_theta = remote(green, theta.at[own_rows], theta_sem.at[0], theta_sem.at[1], sibling)
+    swap_theta = remote(theta.at[own_rows], theta.at[own_rows], theta_sem.at[0], theta_sem.at[1], sibling)
     swap_meta = remote(meta, meta_in, meta_sem.at[0], meta_sem.at[1], sibling)
 
     def entry_out(src, v):
@@ -225,9 +225,9 @@
 
     def enter_on(v):
         entry_in(0, v).wait_recv()
+        for n in range(3):
+            share_out(0, v, n).start()
         entry_on(v).start()
-        for n in range(3):
-            share_out(0, v, n).start()
 
     def gather(v):
         for n in range(3):
@@ -287,13 +287,13 @@
             for v in range(VECS):
                 transit_copy(v).start()
 
-        swap_theta.start()
+        load_theta.start()
         load_slab.start()
-        load_theta.start()
         hail(0)
         prepare()
+        load_theta.wait()
+        swap_theta.start()
         load_slab.wait()
-        load_theta.wait()
         steps = {"t": pass_on, "u": send_on, "e": enter, "s": gather, "w": swapped}
         run(PLAN_0, steps, unit_of(own_units | {"a": (1, mine_base), "b": (1, other_base)}))
 
@@ -301,13 +301,13 @@
     def _():
         for v in range(VECS):
             entry_out(chol.at[v, quarter(cross_color)], v).start()
-        swap_theta.start()
+        load_theta.start()
         load_slab.start()
-        load_theta.start()
         hail(0)
         prepare()
+        load_theta.wait()
+        swap_theta.start()
         load_slab.wait()
-        load_theta.wait()
         steps = {"e": enter_on, "f": second_enter, "s": gather_on, "g": second_gather, "w": swapped}
         run(PLAN_1, steps, unit_of(own_units | {"p": (1, near_base), "q": (2, next_base)}))
 

time: 45 us -> 45 us (level)
  no operation moved by 1% of the time
where the time goes in v7:
time: 45 us; the launch traced here: 44.9 us
  Pallas kernels  43.6 us (97%)
  between operations  1.29 us (3%)
    pallas_call x1, Pallas kernels, body(): pl.pallas_call(kernel, out_shape=jax.ShapeDtypeStruct((8, LANES), jnp.flo...  42.3 us
    pallas_call x1, Pallas kernels, body(): pl.pallas_call(deal, out_shape=(jax.ShapeDtypeStruct((WALKERS_DEV,), jnp....  1.26 us

profile of v7, /device:TPU:1, one launch (start us, length us, event | category | flops | bytes accessed | tf_op | source)
XLA Modules:
  0.0 44.9 jit_solution(5041948643288943916)
XLA Ops:
  1.3 42.3 %walkers.1.tile = f32[8,128]{1,0:T(8,128)} custom-call(bf16[4,256,1024]{2,1,0:T(8,128)(2,1)} %chol.1, bf16[4,1024,256]{2,1,0:T(8,128)(2,1)} %green.1, f32[4,16]{1,0:T(4,128)} %fields_in.1, f32[4]{0:T(128)} %weights_in.1, s32[4]{0:T(128)} %partner_in.1, s32[1,1]{1,0:T(1,128)S(6)} %copy.10.counts), custom_call_target="tpu_custom_call" | custom-call | tf_op jit(solution)/shard_map/walkers/pallas_call | solution.py:430
  43.6 1.3 %deal.1 = (f32[4]{0:T(128)}, f32[4]{0:T(128)}, f32[4,16]{1,0:T(4,128)}, f32[1]{0:T(128)}) custom-call(f32[8,128]{1,0:T(8,128)} %walkers.1.tile), custom_call_target="tpu_custom_call" | custom-call | tf_op jit(solution)/shard_map/deal/pallas_call | solution.py:458
